TPU v7x, 512 devices: a whole 4x8x8 slice. The times are simulated.
512 devices in a mesh: expert: 64 (over x, y, core), head: 8 (over z).
Axes of the slice: x: 4, y: 8, z: 8, core: 2. Of those that a mesh axis runs over, the one named last changes fastest.
Arguments:
- tokens: bfloat16 [2, 1536, 4096], P(None, 'expert', 'head'), may hold values from -6 to 6
- queries: bfloat16 [2, 1536, 64, 576], P(None, 'expert', 'head'), may hold values from -10 to 10
- latent_cache: bfloat16 [1536, 16, 576], P('expert'), may hold values from -4 to 4
- lengths: int32 [1536], P('expert'), may hold values from 2 to 14, as said below
- expert_ids: int32 [2, 1536, 8], P(None, 'expert'), may hold values from 0 to 63, all different within a row; in each aligned block of 24 rows (0 to 23, 24 to 47, ..., all dimensions but the last counted through in order) at most 4 rows name the same one
- route_score: float32 [2, 1536, 8], P(None, 'expert'), may hold values from 0.05 to 1
- survive: int32 [1, 1536], P(None, 'expert'), may hold values 0 or 1
- destination: int32 [1, 1536], P(None, 'expert'), may hold values from 0 to 63, as said below
- w_gate: bfloat16 [64, 4096, 1024], P('expert', None, 'head'), may hold values from -0.09375 to 0.09375
- w_up: bfloat16 [64, 4096, 1024], P('expert', None, 'head'), may hold values from -0.09375 to 0.09375
- w_down: bfloat16 [64, 1024, 4096], P('expert', 'head'), may hold values from -0.1875 to 0.1875
- w_latent: bfloat16 [4096, 576], P('head'), may hold values from -0.09375 to 0.09375
- kv_gain: float32 [512], replicated, may hold values from 0.1 to 1.9
Outputs:
- attn_out: bfloat16 [2, 1536, 64, 512], P(None, 'expert', 'head')
- layer_out: bfloat16 [2, 1536, 4096], P(None, 'expert', 'head')
Inputs may be any that keep to these rules, and one draw needn't show every extreme that they name: `expert_ids`: in the rows of one group at one step no expert is named more than 4 times. `lengths`: counts the current token. `destination`: at each step the rows that share a slot index r in all groups go to distinct groups, so every slot receives exactly one row; at each step, no group sends more than 1 row to any one group.
All inputs are finite; a program needn't handle non-finite values. No bound on the sum of `survive` on one device may be relied on, other than what follows from the above.
Results may differ from a plain program's by a relative error of at most 0.014.
Values may be sent and summed in bfloat16 or wider, within the bound.
No kernel may reach another device: no remote copies, remote signals or barrier semaphores. Data moves between devices by JAX's collectives and lax.ppermute only.
A program may use at most 64 MiB of HBM per device.

v0:
```python
import jax
import jax.numpy as jnp
from jax import lax
from jax.sharding import PartitionSpec as P

KVR = 512
TOPK = 8
STEPS = 2


SCORE_SCALE = 192.0 ** (-0.5)
ROUTE_SCALE = 2.5
NORM_EPS = 1e-06


def slot_table(chosen, bin_count):
    onehot = (chosen[:, None] == jnp.arange(bin_count)[None, :]).astype(jnp.int32)
    before = jnp.cumsum(onehot, axis=0) - onehot
    return jnp.sum(before * onehot, axis=1)


def attend(query, cache_now, lengths_now):
    scores = (
        jnp.einsum("rhc,rpc->rhp", query, cache_now, preferred_element_type=jnp.float32)
        * SCORE_SCALE
    )
    in_range = lax.broadcasted_iota(jnp.int32, scores.shape, 2) < lengths_now[:, None, None]
    row_top = jnp.max(jnp.where(in_range, scores, -1e30), axis=2, keepdims=True)
    exp_terms = jnp.where(in_range, jnp.exp(scores - row_top), 0.0)
    denominator = jnp.sum(exp_terms, axis=2, keepdims=True)
    denominator = jnp.where(lengths_now[:, None, None] > 0, denominator, 1.0)
    weights = (exp_terms / denominator).astype(jnp.bfloat16)
    values = cache_now[:, :, :KVR]
    return jnp.einsum("rhp,rpc->rhc", weights, values, preferred_element_type=jnp.float32).astype(
        jnp.bfloat16
    )


def migrate_rows(cache_now, lengths_now, target, alive, groups, movers):
    row_count, position_count, latent_width = cache_now.shape
    slot_flat = target * movers + slot_table(target, groups)
    spread = (slot_flat[:, None] == jnp.arange(groups * movers)[None, :]).astype(jnp.float32)
    row_info = jnp.stack([jnp.arange(row_count) + 1, alive * lengths_now], axis=1).astype(
        jnp.float32
    )
    labels_out = (
        jnp.einsum("rs,rc->sc", spread, row_info, precision=lax.Precision.HIGHEST)
        .astype(jnp.bfloat16)
        .reshape(groups, movers, 2)
    )
    packed = jnp.einsum(
        "rs,rx->sx",
        spread.astype(jnp.bfloat16),
        cache_now.reshape(row_count, position_count * latent_width),
        preferred_element_type=jnp.float32,
    ).astype(jnp.bfloat16)
    packed = packed.reshape(groups, movers, position_count, latent_width)
    arrived, labels = (
        lax.all_to_all(packed, "expert", split_axis=0, concat_axis=0, tiled=True),
        lax.all_to_all(labels_out, "expert", split_axis=0, concat_axis=0, tiled=True),
    )
    labels = labels.reshape(-1, 2).astype(jnp.float32)
    wanted = (jnp.arange(row_count) + 1).astype(jnp.float32)
    choose = (labels[None, :, 0] == wanted[:, None]).astype(jnp.float32)
    cache_new = jnp.dot(
        choose.astype(jnp.bfloat16),
        arrived.reshape(-1, position_count * latent_width),
        preferred_element_type=jnp.float32,
    )
    cache_new = cache_new.astype(jnp.bfloat16).reshape(row_count, position_count, latent_width)
    lengths_new = jnp.dot(choose, labels[:, 1], precision=lax.Precision.HIGHEST).astype(jnp.int32)
    return (cache_new, lengths_new)


def on_device(
    tokens,
    queries,
    latent_cache,
    lengths,
    expert_ids,
    route_score,
    survive,
    destination,
    w_gate,
    w_up,
    w_down,
    w_latent,
    kv_gain,
):
    groups = lax.axis_size("expert")
    row_count = latent_cache.shape[0]
    slice_width = tokens.shape[2]
    capacity = max(2, (4 * TOPK * row_count + 3 * groups - 1) // (3 * groups))
    movers = (row_count + groups - 1) // groups
    cache_now = latent_cache
    lengths_now = lengths
    attended = []
    layered = []
    for section_index in range(STEPS):
        attended.append(attend(queries[section_index], cache_now, lengths_now))
        chosen = expert_ids[section_index].reshape(-1)
        slot_flat = chosen * capacity + slot_table(chosen, groups)
        onehot = (slot_flat[:, None] == jnp.arange(groups * capacity)[None, :]).astype(jnp.int32)
        spread = jnp.sum(onehot.reshape(row_count, TOPK, groups * capacity), axis=1).astype(
            jnp.bfloat16
        )
        sending = jnp.einsum(
            "rs,rd->sd", spread, tokens[section_index], preferred_element_type=jnp.float32
        ).astype(jnp.bfloat16)
        arrived = lax.all_to_all(
            sending.reshape(groups, capacity, slice_width),
            "expert",
            split_axis=0,
            concat_axis=0,
            tiled=True,
        )
        arrived = arrived.reshape(groups * capacity, slice_width)
        shard_piece = lax.all_gather(arrived, "head", axis=1, tiled=True)
        gate_rows = w_gate[0]
        up_rows = w_up[0]
        gate_acts = jnp.dot(shard_piece, gate_rows, preferred_element_type=jnp.float32)
        up_acts = jnp.dot(shard_piece, up_rows, preferred_element_type=jnp.float32)
        hidden = (jax.nn.silu(gate_acts) * up_acts).astype(jnp.bfloat16)
        down_terms = jnp.dot(hidden, w_down[0], preferred_element_type=jnp.float32)
        summed = lax.psum_scatter(
            down_terms.astype(jnp.bfloat16), "head", scatter_dimension=1, tiled=True
        )
        answers = summed.reshape(groups, capacity, slice_width)
        returned = lax.all_to_all(
            answers, "expert", split_axis=0, concat_axis=0, tiled=True
        ).reshape(groups * capacity, slice_width)
        picked = returned[slot_flat].reshape(row_count, TOPK, slice_width)
        share_raw = route_score[section_index]
        route_weight = ROUTE_SCALE * share_raw / jnp.sum(share_raw, axis=1, keepdims=True)
        mixed_out = tokens[section_index].astype(jnp.float32) + jnp.einsum(
            "rk,rkd->rd", route_weight, picked.astype(jnp.float32), precision=lax.Precision.HIGHEST
        )
        layer_row = mixed_out.astype(jnp.bfloat16)
        layered.append(layer_row)
        if section_index + 1 < STEPS:
            partial_value = jnp.dot(layer_row, w_latent, preferred_element_type=jnp.float32)
            whole_sum = lax.psum(partial_value.astype(jnp.bfloat16), "head").astype(jnp.float32)
            leading = whole_sum[:, :KVR]
            norm_scale = lax.rsqrt(jnp.mean(leading * leading, axis=1, keepdims=True) + NORM_EPS)
            latent = jnp.concatenate(
                [leading * norm_scale * kv_gain, whole_sum[:, KVR:]], axis=1
            ).astype(jnp.bfloat16)
            at_length = (
                lax.broadcasted_iota(jnp.int32, cache_now.shape, 1) == lengths_now[:, None, None]
            )
            cache_now = jnp.where(at_length, latent[:, None, :], cache_now)
            lengths_now = lengths_now + 1
            cache_now, lengths_now = migrate_rows(
                cache_now,
                lengths_now,
                destination[section_index],
                survive[section_index],
                groups,
                movers,
            )
    return (jnp.stack(attended), jnp.stack(layered))


def solution(mesh):
    return jax.shard_map(
        on_device,
        mesh=mesh,
        in_specs=(
            P(None, "expert", "head"),
            P(None, "expert", "head", None),
            P("expert", None, None),
            P("expert"),
            P(None, "expert", None),
            P(None, "expert", None),
            P(None, "expert"),
            P(None, "expert"),
            P("expert", None, "head"),
            P("expert", None, "head"),
            P("expert", "head", None),
            P("head", None),
            P(),
        ),
        out_specs=(P(None, "expert", "head", None), P(None, "expert", "head")),
        check_vma=False,
    )
```

profile of v0, /device:TPU:1, one launch (start us, length us, event | category | flops | bytes accessed | tf_op | source)
XLA Modules:
  0.0 338.6 jit_solution(2399740661019613438)
XLA Ops:
  7.2 0.8 fusion.95
  8.1 0.1 eq.137
  8.2 0.6 reduce-window.14
  8.8 0.2 slice_reduce_fusion.1
  9.1 0.1 bitcast_bitcast_fusion.1
  9.3 0.1 convert_reduce_fusion.1
  9.4 1.0 convolution_convert_fusion.5
  10.5 23.4 %all_to_all.30 = bf16[64,4,512]{2,1,0:T(4,128)(2,1)S(1)} all-to-all(bf16[64,4,512]{2,1,0:T(4,128)(2,1)S(1)} %reshape.267), channel_id=1, replica_groups=mesh['expert'=64,'head'=8] {'expert'}, dimensions={0} | all-to-all | bytes 524288 | tf_op jit(solution)/shard_map/all_to_all | solution.py:110
  33.9 0.8 reshape.268
  35.0 0.6 reduce-window.16
  35.6 0.2 slice_reduce_fusion
  35.8 0.1 bitcast_bitcast_fusion
  36.0 0.5 copy-done.14
  36.5 0.1 convert_reduce_fusion
  36.7 0.3 convolution_convert_fusion.4
  37.0 17.8 %all_to_all.31 = bf16[64,4,512]{2,1,0:T(4,128)(2,1)S(1)} all-to-all(bf16[64,4,512]{2,1,0:T(4,128)(2,1)S(1)} %reshape.278), channel_id=1, replica_groups=mesh['expert'=64,'head'=8] {'expert'}, dimensions={0} | all-to-all | bytes 524288 | tf_op jit(solution)/shard_map/all_to_all | solution.py:110
  54.8 0.8 reshape.279
  55.7 19.7 %all-gather.3.cloned.1.call-done = bf16[256,4096]{1,0:T(8,128)(2,1)} async-done(((bf16[256,512]{1,0:T(8,128)(2,1)}), bf16[256,4096]{1,0:T(8,128)(2,1)}) %all-gather.3.cloned.1.call-update) | async-done | bytes 2097168 | tf_op jit(solution)/shard_map/all_gather | solution.py:118
  75.4 2.7 fusion.23
  78.1 3.9 %convolution_convert_fusion.3 = bf16[256,4096]{1,0:T(8,128)(2,1)} fusion(bf16[256,4096]{1,0:T(8,128)(2,1)S(1)} %copy-done.1, bf16[1,128,4096]{2,1,0:T(8,128)(2,1)S(1)} %copy-done, bf16[1,4096,128]{2,1,0:T(8,128)(2,1)} %param.22, f32[256,128]{1,0:T(8,128)S(1)} %fusion.23), kind=kOutput, calls=%fused_computation.7 | convolution fusion | flops 538116096 | bytes 6422528 | tf_op jit(solution)/shard_map/dot_general | solution.py:124
  82.1 38.2 %all-gather.5.cloned.1.call-done = bf16[256,4096]{1,0:T(8,128)(2,1)} async-done(((bf16[256,512]{1,0:T(8,128)(2,1)}), bf16[256,4096]{1,0:T(8,128)(2,1)}) %all-gather.5.cloned.1.call-update) | async-done | bytes 2097168 | tf_op jit(solution)/shard_map/all_gather | solution.py:118
  120.2 2.7 fusion.21
  123.0 3.8 %convolution_convert_fusion.2 = bf16[256,4096]{1,0:T(8,128)(2,1)} fusion(bf16[256,4096]{1,0:T(8,128)(2,1)S(1)} %copy-done.2, bf16[1,128,4096]{2,1,0:T(8,128)(2,1)S(1)} %copy-done, bf16[1,4096,128]{2,1,0:T(8,128)(2,1)} %param.22, f32[256,128]{1,0:T(8,128)S(1)} %fusion.21), kind=kOutput, calls=%fused_computation.6 | convolution fusion | flops 538116096 | bytes 6422528 | tf_op jit(solution)/shard_map/dot_general | solution.py:124
  126.9 0.6 copy-done.12
  127.5 0.6 fusion.82
  128.2 0.7 mul.128
  129.0 0.2 select_reduce_fusion.2
  129.2 37.4 %reduce-scatter.3.cloned.1.call-done = bf16[256,512]{1,0:T(8,128)(2,1)} async-done(((bf16[256,4096]{1,0:T(8,128)(2,1)}), bf16[256,512]{1,0:T(8,128)(2,1)}) %reduce-scatter.3.cloned.1.call-update) | async-done | bytes 262160 | tf_op jit(solution)/shard_map/reduce_scatter | solution.py:125
  166.6 1.7 reshape.269
  168.3 14.6 %all-to-all-start.2 = ((bf16[64,4,512]{2,1,0:T(4,128)(2,1)}), bf16[64,4,512]{2,1,0:T(4,128)(2,1)S(1)}, u32[]{:S(2)}, u32[]{:S(2)}) async-start(bf16[64,4,512]{2,1,0:T(4,128)(2,1)} %reshape.269), calls=%async_computation.3 | async-start | bytes 524288 | tf_op jit(solution)/shard_map/all_to_all | solution.py:129
  183.0 0.2 fusion.14
  183.2 0.7 copy.32
  183.9 29.1 %reduce-scatter.5.cloned.1.call-done = bf16[256,512]{1,0:T(8,128)(2,1)} async-done(((bf16[256,4096]{1,0:T(8,128)(2,1)}), bf16[256,512]{1,0:T(8,128)(2,1)}) %reduce-scatter.5.cloned.1.call-update) | async-done | bytes 262160 | tf_op jit(solution)/shard_map/reduce_scatter | solution.py:125
  213.0 1.7 reshape.280
  214.7 15.0 %all-to-all-start = ((bf16[64,1,2]{2,1,0:T(2,128)(2,1)}), bf16[64,1,2]{2,1,0:T(2,128)(2,1)S(1)}, u32[]{:S(2)}, u32[]{:S(2)}) async-start(bf16[64,1,2]{2,1,0:T(2,128)(2,1)} %copy.32), calls=%async_computation | async-start | bytes 65536 | tf_op jit(solution)/shard_map/all_to_all | solution.py:60
  229.8 1.0 gather_fusion
  230.8 0.3 fusion.34
  231.1 0.3 convolution_convert_fusion.8
  231.4 21.5 %psum.7 = bf16[24,576]{1,0:T(8,128)(2,1)S(1)} all-reduce(bf16[24,576]{1,0:T(8,128)(2,1)S(1)} %convolution_convert_fusion.8), channel_id=1, replica_groups=mesh['expert'=64,'head'=8] {'head'}, use_global_device_ids=true, to_apply=%region_10.11 | all-reduce | flops 13824 | bytes 55296 | tf_op jit(solution)/shard_map/psum | solution.py:142
  252.9 0.1 fusion.54
  253.1 16.7 %all-to-all-start.5 = ((bf16[64,4,512]{2,1,0:T(4,128)(2,1)}), bf16[64,4,512]{2,1,0:T(4,128)(2,1)S(1)}, u32[]{:S(2)}, u32[]{:S(2)}) async-start(bf16[64,4,512]{2,1,0:T(4,128)(2,1)} %reshape.280), calls=%async_computation.7 | async-start | bytes 524288 | tf_op jit(solution)/shard_map/all_to_all | solution.py:129
  269.8 0.2 fusion.25
  270.0 0.4 reshape.272
  270.4 0.6 convolution_convert_fusion
  271.0 2.0 reshape.273
  273.0 8.8 %all-to-all-done.5 = bf16[64,4,512]{2,1,0:T(4,128)(2,1)S(1)} async-done(((bf16[64,4,512]{2,1,0:T(4,128)(2,1)}), bf16[64,4,512]{2,1,0:T(4,128)(2,1)S(1)}, u32[]{:S(2)}, u32[]{:S(2)}) %all-to-all-start.5) | async-done | bytes 262176 | tf_op jit(solution)/shard_map/all_to_all | solution.py:129
  281.8 6.2 %all-to-all-start.3 = ((bf16[64,1,16,576]{3,2,1,0:T(8,128)(2,1)}), bf16[64,1,16,576]{3,2,1,0:T(8,128)(2,1)S(1)}, u32[]{:S(2)}, u32[]{:S(2)}) async-start(bf16[64,1,16,576]{3,2,1,0:T(8,128)(2,1)} %bitcast.22), calls=%async_computation.4 | async-start | bytes 2621440 | tf_op jit(solution)/shard_map/all_to_all | solution.py:59
  288.1 1.2 convolution_multiply_fusion.3
  289.4 5.5 %fusion.97 = (f32[24,8]{1,0:T(8,128)S(1)}, f32[24,8,16]{2,1,0:T(8,128)S(1)}) fusion(f32[24,8,16]{2,1,0:T(8,128)S(1)} %convolution_multiply_fusion.3, s32[24]{0:T(128)S(1)} %copy-done.20), kind=kOutput, calls=%fused_computation.172 | output fusion | flops 18447 | bytes 25440 | tf_op jit(solution)/shard_map/sub | solution.py:29
  294.9 1.1 fusion.2
  296.0 0.1 copy.33
  296.1 0.8 broadcast_compare_fusion
  296.9 1.0 gather_fusion.1
  298.0 0.3 fusion.32
  298.3 0.6 pad_maximum_fusion.1
  299.0 23.2 %all-to-all-done.3 = bf16[64,1,16,576]{3,2,1,0:T(8,128)(2,1)S(1)} async-done(((bf16[64,1,16,576]{3,2,1,0:T(8,128)(2,1)}), bf16[64,1,16,576]{3,2,1,0:T(8,128)(2,1)S(1)}, u32[]{:S(2)}, u32[]{:S(2)}) %all-to-all-start.3) | async-done | bytes 1179680 | tf_op jit(solution)/shard_map/all_to_all | solution.py:59
  322.1 1.1 reshape.274
  323.3 0.3 convolution_convert_fusion.1
  323.7 0.4 reshape.275
  324.1 1.2 fusion.12
  325.3 5.5 %fusion.96 = (f32[24,8]{1,0:T(8,128)S(1)}, f32[24,8,16]{2,1,0:T(8,128)S(1)}) fusion(f32[24,8,16]{2,1,0:T(8,128)S(1)} %fusion.12, s32[24]{0:T(128)S(1)} %copy-done.27), kind=kOutput, calls=%fused_computation.171 | output fusion | flops 18447 | bytes 25440 | tf_op jit(solution)/shard_map/sub | solution.py:29
  330.8 0.1 broadcast_select_fusion
  330.9 0.3 fusion.3
  331.3 0.8 pad_maximum_fusion
  (109 shorter events, 1.9 us)
Async XLA Ops:
  7.2 70.9 %copy-start = (bf16[1,128,4096]{2,1,0:T(8,128)(2,1)S(1)}, bf16[1,128,4096]{2,1,0:T(8,128)(2,1)}, u32[]{:S(2)}) copy-start(bf16[1,128,4096]{2,1,0:T(8,128)(2,1)} %param.23) | copy-start | bytes 3145732
  7.2 29.5 %copy-start.7 = (bf16[2,24,512]{2,1,0:T(8,128)(2,1)S(1)}, bf16[2,24,512]{2,1,0:T(8,128)(2,1)}, u32[]{:S(2)}) copy-start(bf16[2,24,512]{2,1,0:T(8,128)(2,1)} %param.13) | copy-start | bytes 147460
  7.2 68.2 %all-gather.3.cloned.1.call-start = ((), (), s32[]{:S(2)}) async-start(), calls=%async_computation.8 | async-start | bytes 2359296 | tf_op jit(solution)/shard_map/all_gather | solution.py:118
  34.7 85.5 %all-gather.5.cloned.1.call-start = ((), (), s32[]{:S(2)}) async-start(), calls=%async_computation.10 | async-start | bytes 2359296 | tf_op jit(solution)/shard_map/all_gather | solution.py:118
  35.9 0.6 copy-start.14
  55.6 111.0 %reduce-scatter.3.cloned.1.call-start = ((), (), s32[]{:S(2)}) async-start(), calls=%async_computation.9 | async-start | bytes 2359296 | tf_op jit(solution)/shard_map/reduce_scatter | solution.py:125
  75.4 2.7 copy-start.1
  82.0 130.9 %reduce-scatter.5.cloned.1.call-start = ((), (), s32[]{:S(2)}) async-start(), calls=%async_computation.11 | async-start | bytes 2359296 | tf_op jit(solution)/shard_map/reduce_scatter | solution.py:125
  120.2 2.7 copy-start.2
  126.8 0.7 copy-start.12
  126.8 2.1 copy-start.18
  126.8 2.4 copy-start.19
  126.8 2.4 copy-start.26
  129.2 101.9 %copy-start.4 = (bf16[512,576]{0,1:T(8,128)(2,1)S(1)}, bf16[512,576]{0,1:T(8,128)(2,1)}, u32[]{:S(2)}) copy-start(bf16[512,576]{0,1:T(8,128)(2,1)} %param.24) | copy-start | bytes 1769476
  168.3 46.4 %all-to-all-start.2 = ((bf16[64,4,512]{2,1,0:T(4,128)(2,1)}), bf16[64,4,512]{2,1,0:T(4,128)(2,1)S(1)}, u32[]{:S(2)}, u32[]{:S(2)}) async-start(bf16[64,4,512]{2,1,0:T(4,128)(2,1)} %reshape.269), calls=%async_computation.3 | async-start | bytes 524288 | tf_op jit(solution)/shard_map/all_to_all | solution.py:129
  182.9 70.1 %copy-start.17 = (f32[512]{0:T(512)S(1)}, f32[512]{0:T(512)}, u32[]{:S(2)}) copy-start(f32[512]{0:T(512)} %param.25) | copy-start | bytes 6148
  214.7 55.1 %copy-start.3 = (bf16[24,16,576]{2,1,0:T(8,128)(2,1)S(1)}, bf16[24,16,576]{2,1,0:T(8,128)(2,1)}, u32[]{:S(2)}) copy-start(bf16[24,16,576]{2,1,0:T(8,128)(2,1)} %param.15) | copy-start | bytes 1327108
  214.7 38.4 %all-to-all-start = ((bf16[64,1,2]{2,1,0:T(2,128)(2,1)}), bf16[64,1,2]{2,1,0:T(2,128)(2,1)S(1)}, u32[]{:S(2)}, u32[]{:S(2)}) async-start(bf16[64,1,2]{2,1,0:T(2,128)(2,1)} %copy.32), calls=%async_computation | async-start | bytes 65536 | tf_op jit(solution)/shard_map/all_to_all | solution.py:60
  231.1 38.7 %copy-start.5 = (f32[24,1,512]{2,1,0:T(1,128)}, f32[24,1,512]{2,1,0:T(1,128)S(1)}, u32[]{:S(2)}) copy-start(f32[24,1,512]{2,1,0:T(1,128)S(1)} %fusion.34) | copy-start | bytes 147460
  253.1 16.9 %copy-start.10 = (bf16[64,1,2]{2,1,0:T(2,128)(2,1)}, bf16[64,1,2]{2,1,0:T(2,128)(2,1)S(1)}, u32[]{:S(2)}) copy-start(bf16[64,1,2]{2,1,0:T(2,128)(2,1)S(1)} %all-to-all-done) | copy-start | bytes 772
  253.1 28.7 %all-to-all-start.5 = ((bf16[64,4,512]{2,1,0:T(4,128)(2,1)}), bf16[64,4,512]{2,1,0:T(4,128)(2,1)S(1)}, u32[]{:S(2)}, u32[]{:S(2)}) async-start(bf16[64,4,512]{2,1,0:T(4,128)(2,1)} %reshape.280), calls=%async_computation.7 | async-start | bytes 524288 | tf_op jit(solution)/shard_map/all_to_all | solution.py:129
  271.0 17.0 %copy-start.15 = (s32[192]{0:T(256)S(1)}, s32[192]{0:T(256)}, u32[]{:S(2)}) copy-start(s32[192]{0:T(256)} %copy-done.14) | copy-start | bytes 2308
  271.0 17.0 %copy-start.16 = (s32[192,1]{0,1:T(1,128)S(1)}, s32[192,1]{0,1:T(1,128)}, u32[]{:S(2)}) copy-start(s32[192,1]{0,1:T(1,128)} %mul.128) | copy-start | bytes 2308
  271.0 17.0 %copy-start.13 = (f32[24,8,1]{0,1,2:T(8,128)S(1)}, f32[24,8,1]{0,1,2:T(8,128)}, u32[]{:S(2)}) copy-start(f32[24,8,1]{0,1,2:T(8,128)} %get-tuple-element.8) | copy-start | bytes 2308
  271.0 17.1 %copy-start.20 = (s32[24]{0:T(128)S(1)}, s32[24]{0:T(128)}, u32[]{:S(2)}) copy-start(s32[24]{0:T(128)} %param.16) | copy-start | bytes 292
  281.8 14.2 %copy-start.11 = (bf16[64,1,2]{2,1,0:T(2,128)(2,1)S(1)}, bf16[64,1,2]{2,1,0:T(2,128)(2,1)}, u32[]{:S(2)}) copy-start(bf16[64,1,2]{2,1,0:T(2,128)(2,1)} %copy-done.10) | copy-start | bytes 772
  281.8 40.3 %all-to-all-start.3 = ((bf16[64,1,16,576]{3,2,1,0:T(8,128)(2,1)}), bf16[64,1,16,576]{3,2,1,0:T(8,128)(2,1)S(1)}, u32[]{:S(2)}, u32[]{:S(2)}) async-start(bf16[64,1,16,576]{3,2,1,0:T(8,128)(2,1)} %bitcast.22), calls=%async_computation.4 | async-start | bytes 2621440 | tf_op jit(solution)/shard_map/all_to_all | solution.py:59
  288.1 9.9 %copy-start.21 = (f32[24]{0:T(128)}, f32[24]{0:T(128)S(1)}, u32[]{:S(2)}) copy-start(f32[24]{0:T(128)S(1)} %add_convert_fusion.2) | copy-start | bytes 292
  288.1 10.2 %copy-start.6 = (f32[24,1,512]{2,1,0:T(1,128)S(1)}, f32[24,1,512]{2,1,0:T(1,128)}, u32[]{:S(2)}) copy-start(f32[24,1,512]{2,1,0:T(1,128)} %copy-done.5) | copy-start | bytes 147460
  288.1 10.2 %copy-start.8 = (bf16[2,24,512]{2,1,0:T(8,128)(2,1)S(1)}, bf16[2,24,512]{2,1,0:T(8,128)(2,1)}, u32[]{:S(2)}) copy-start(bf16[2,24,512]{2,1,0:T(8,128)(2,1)} %param.13) | copy-start | bytes 147460
  296.1 2.9 copy-start.23
  298.3 25.0 %copy-start.22 = (f32[24]{0:T(128)S(1)}, f32[24]{0:T(128)}, u32[]{:S(2)}) copy-start(f32[24]{0:T(128)} %copy-done.21) | copy-start | bytes 292
  322.1 1.1 copy-start.24
  323.3 2.0 copy-start.27
  323.3 7.5 %copy-start.25 = (pred[24]{0:T(512)(128)(4,1)S(1)}, pred[24]{0:T(512)(128)(4,1)}, u32[]{:S(2)}) copy-start(pred[24]{0:T(512)(128)(4,1)} %get-tuple-element.12) | copy-start | bytes 76
  323.3 8.0 %copy-start.9 = (bf16[1,24,8,512]{3,2,1,0:T(8,128)(2,1)S(1)}, bf16[1,24,8,512]{3,2,1,0:T(8,128)(2,1)}, u32[]{:S(2)}) copy-start(bf16[1,24,8,512]{3,2,1,0:T(8,128)(2,1)} %fusion.2) | copy-start | bytes 589828
Sparse Core Ops, SparseCore 0:
  34.8 40.5 all-gather.2
  77.5 42.7 all-gather.4
  123.1 43.4 reduce-scatter.2
  169.3 43.6 reduce-scatter.4
where the time goes:
time: 339 us
  waiting for transfers between devices  156 us (46%)
  blocking collectives  62.8 us (19%)
  starting transfers between devices  52.6 us (16%)
  matrix products  20.9 us (6%)
  other arithmetic  15.9 us (5%)
  local copies, waits for them, and re-layouts  15.6 us (5%)
  between operations  14.4 us (4%)
    reduce_scatter x2, waiting for transfers between devices, on_device(): lax.psum_scatter(down_terms.astype(jnp.bfloat16), 'head', scatter_dimensi...  66.4 us
    all_gather x2, waiting for transfers between devices, on_device(): shard_piece = lax.all_gather(arrived, 'head', axis=1, tiled=True)  57.9 us
    all_to_all x2, blocking collectives, on_device(): lax.all_to_all(sending.reshape(groups, capacity, slice_width), 'expert',...  41.2 us
    all_to_all x2, starting transfers between devices, on_device(): lax.all_to_all(answers, 'expert', split_axis=0, concat_axis=0, tiled=True)  31.3 us
    all_to_all x1, waiting for transfers between devices, migrate_rows(): lax.all_to_all(packed, 'expert', split_axis=0, concat_axis=0, tiled=True)  23.2 us
    psum x1, blocking collectives, on_device(): lax.psum(partial_value.astype(jnp.bfloat16), 'head').astype(jnp.float32)  21.5 us
    all_to_all x1, starting transfers between devices, migrate_rows(): lax.all_to_all(labels_out, 'expert', split_axis=0, concat_axis=0, tiled=T...  15 us
    sub x2, other arithmetic, attend(): exp_terms = jnp.where(in_range, jnp.exp(scores - row_top), 0.0)  11 us
  transfers between devices with their start and end apart: 8, of which 6 were waited for; matrix products, arithmetic and copies ran while one was open for 11% of the time, Pallas kernels for 0%

commit v1 on v0

v1 whole, which is shorter than its diff:
```python
import jax
import jax.numpy as jnp
from jax import lax
from jax.sharding import PartitionSpec as P

KVR = 512
TOPK = 8
STEPS = 2
CAP = 4

SCORE_SCALE = 192.0 ** (-0.5)
ROUTE_SCALE = 2.5
NORM_EPS = 1e-06
LOW = -1e30

BF = jnp.bfloat16
F32 = jnp.float32


def dot(a, b, dims, precision=None):
    return lax.dot_general(a, b, (dims, ((), ())), precision=precision, preferred_element_type=F32)


def exchange(x, axis):
    return lax.all_to_all(x, axis, split_axis=0, concat_axis=0, tiled=True)


def together(*arrays):
    return lax.optimization_barrier(arrays)


def routing(ids, score, groups):
    rows = ids.shape[0]
    column = lax.broadcasted_iota(jnp.int32, (1, 1, groups * CAP), 2)
    hit = ids[:, :, None] == column // CAP
    named = jnp.any(hit, axis=1)
    share = ROUTE_SCALE * score / jnp.sum(score, axis=1, keepdims=True)
    weight = jnp.sum(jnp.where(hit, share[:, :, None], 0.0), axis=1)
    earlier = (
        lax.broadcasted_iota(jnp.int32, (rows, rows), 1)
        < lax.broadcasted_iota(jnp.int32, (rows, rows), 0)
    ).astype(BF)
    before = dot(earlier, named.astype(BF), ((1,), (0,)))
    place = named & (before == (column[0] % CAP).astype(F32))
    return place.astype(BF), jnp.where(place, weight, 0.0)


def softmax_values(parts):
    top = parts[0][0].max(axis=1, keepdims=True)
    for scores, _, _ in parts[1:]:
        top = jnp.maximum(top, scores.max(axis=1, keepdims=True))
    terms = [jnp.where(mask, jnp.exp(scores - top), 0.0) for scores, mask, _ in parts]
    total = sum(t.sum(axis=1, keepdims=True) for t in terms)
    total = jnp.where(total > 0, total, 1.0)
    return sum(
        dot((t / total).astype(BF), values, ((1,), (0,)))
        for t, (_, _, values) in zip(terms, parts)
    )


def on_device(
    tokens,
    queries,
    latent_cache,
    lengths,
    expert_ids,
    route_score,
    survive,
    destination,
    w_gate,
    w_up,
    w_down,
    w_latent,
    kv_gain,
):
    groups = lax.axis_size("expert")
    heads_axis = lax.axis_size("head")
    rows, positions, width = latent_cache.shape
    heads = queries.shape[2]
    feats = tokens.shape[2]
    block = w_gate.shape[2]
    wide = 768

    route = [routing(expert_ids[s], route_score[s], groups) for s in range(STEPS)]

    def send(s):
        return dot(route[s][0], tokens[s], ((0,), (0,))).astype(BF)

    arrived0 = exchange(send(0).reshape(groups, CAP, feats), "expert")
    rows0 = lax.all_gather(arrived0.reshape(groups * CAP, feats), "head", axis=1, tiled=True)

    down_slices = w_down[0].reshape(block, heads_axis, feats).transpose(1, 0, 2)
    down_slices, arrived0 = together(down_slices, arrived0)
    down = exchange(down_slices, "head").reshape(heads_axis * block, feats)

    alive = survive[0] == 1
    eye = jnp.eye(rows, wide - width, dtype=BF)
    target = (destination[0][:, None] == jnp.arange(groups)[None, :]).astype(BF)
    share = positions // heads_axis
    first = lax.axis_index("head") * share
    held = lax.dynamic_slice_in_dim(latent_cache, first, share, axis=1)
    spot = first + lax.broadcasted_iota(jnp.int32, (rows, share), 1)
    valid = ((spot < lengths[:, None]) & alive[:, None]).astype(BF)
    marked = jnp.concatenate([held, valid[:, :, None] * eye[:, None, :]], axis=2)
    packed = dot(target, marked.reshape(rows, share * wide), ((0,), (0,))).astype(BF)
    piece = share * wide // CAP
    both = jnp.concatenate(
        [send(1).reshape(groups, CAP, feats), packed.reshape(groups, CAP, piece)], axis=2
    )
    both, down = together(both, down)
    both = exchange(both, "expert")
    rows1 = lax.all_gather(
        both[:, :, :feats].reshape(groups * CAP, feats), "head", axis=1, tiled=True
    )
    pieces = both[:, :, feats:].reshape(groups * CAP, piece)
    pieces, rows1 = together(pieces, rows1)
    moved = lax.all_gather(pieces, "head", axis=0, tiled=True)
    moved = moved.reshape(heads_axis * groups * share, wide)

    q0 = queries[0].reshape(rows * heads, width)
    keys0 = latent_cache.reshape(rows * positions, width)
    row_of = lax.broadcasted_iota(jnp.int32, (rows, 1, rows, positions), 0)
    key_of = lax.broadcasted_iota(jnp.int32, (rows, 1, rows, positions), 2)
    spot = lax.broadcasted_iota(jnp.int32, (rows, 1, rows, positions), 3)
    mask0 = (row_of == key_of) & (spot < lengths[:, None, None, None])
    mask0 = jnp.broadcast_to(mask0, (rows, heads, rows, positions)).reshape(
        rows * heads, rows * positions
    )
    scores0 = jnp.where(mask0, dot(q0, keys0, ((1,), (1,))) * SCORE_SCALE, LOW)
    attn0 = softmax_values([(scores0, mask0, keys0[:, :KVR])]).astype(BF)

    def hidden_of(x):
        gate = jnp.dot(x, w_gate[0], preferred_element_type=F32)
        up = jnp.dot(x, w_up[0], preferred_element_type=F32)
        return (jax.nn.silu(gate) * up).astype(BF)

    def everywhere(x):
        return exchange(jnp.broadcast_to(x[None], (heads_axis,) + x.shape), "head")

    def down_of(parts):
        whole = parts.transpose(1, 0, 2).reshape(groups * CAP, heads_axis * block)
        return jnp.dot(whole, down, preferred_element_type=F32).astype(BF).reshape(groups, CAP, feats)

    def combine(s, back):
        back = back.reshape(groups * CAP, feats).astype(F32)
        mixed = dot(route[s][1], back, ((1,), (0,)), precision=lax.Precision.HIGHEST)
        return (tokens[s].astype(F32) + mixed).astype(BF)

    layer0 = combine(0, exchange(down_of(everywhere(hidden_of(rows0))), "expert"))

    part = jnp.dot(layer0, w_latent, preferred_element_type=F32).astype(BF)
    lanes = 128
    chunks = -(-width // lanes)
    part = jnp.pad(part, ((0, 0), (0, chunks * lanes - width)))
    part = [part[:, c * lanes : (c + 1) * lanes] for c in range(chunks)]
    shared = everywhere(jnp.concatenate([hidden_of(rows1)] + part, axis=0))
    sums = shared[:, groups * CAP :].astype(F32).sum(axis=0)
    whole_sum = jnp.concatenate([sums[c * rows : (c + 1) * rows] for c in range(chunks)], axis=1)
    leading = whole_sum[:, :KVR]
    norm = lax.rsqrt(jnp.mean(leading * leading, axis=1, keepdims=True) + NORM_EPS)
    latent = jnp.concatenate(
        [
            (leading * norm * kv_gain).astype(BF),
            whole_sum[:, KVR:width].astype(BF),
            alive.astype(BF)[:, None] * eye,
        ],
        axis=1,
    )
    sent = dot(target, jnp.pad(latent, ((0, 0), (0, 1024 - wide))), ((0,), (0,))).astype(BF)
    answers1 = down_of(shared[:, : groups * CAP])
    last = exchange(
        jnp.concatenate([answers1, sent.reshape(groups, CAP, 1024 // CAP)], axis=2), "expert"
    )
    layer1 = combine(1, last[:, :, :feats])
    fresh = last[:, :, feats:].reshape(groups, 1024)[:, :wide]

    q1 = queries[1].reshape(rows * heads, width)
    eye = jnp.repeat(eye, heads, axis=0)
    parts = []
    for keys in (moved, fresh):
        mask = dot(eye, keys[:, width:], ((1,), (1,))) > 0.5
        scores = dot(q1, keys[:, :width], ((1,), (1,))) * SCORE_SCALE
        parts.append((jnp.where(mask, scores, LOW), mask, keys[:, :KVR]))
    attn1 = softmax_values(parts).astype(BF)

    attn = jnp.stack([attn0, attn1]).reshape(STEPS, rows, heads, KVR)
    return attn, jnp.stack([layer0, layer1])


def solution(mesh):
    return jax.shard_map(
        on_device,
        mesh=mesh,
        in_specs=(
            P(None, "expert", "head"),
            P(None, "expert", "head", None),
            P("expert", None, None),
            P("expert"),
            P(None, "expert", None),
            P(None, "expert", None),
            P(None, "expert"),
            P(None, "expert"),
            P("expert", None, "head"),
            P("expert", None, "head"),
            P("expert", "head", None),
            P("head", None),
            P(),
        ),
        out_specs=(P(None, "expert", "head", None), P(None, "expert", "head")),
        check_vma=False,
    )
```

time: 339 us -> 236 us (0.70)
  waiting for transfers between devices: 156 us -> 80.7 us
  starting transfers between devices: 52.6 us -> 25.4 us
  blocking collectives: 62.8 us -> 71.4 us
  other arithmetic: 15.9 us -> 8.13 us
    reduce_scatter x2 -> x0, waiting for transfers between devices: 66.4 us -> none  [on_device(): lax.psum_scatter(down_terms.astype(jnp.bfloat16), 'head', scatter_dimensi...]
    all_gather x2 -> x3, waiting for transfers between devices: 57.9 us -> 0.06 us  [the longest x1 0.02 us: on_device(): moved = lax.all_gather(pieces, 'head', axis=0, tiled=True)]
    all_to_all x4, waiting for transfers between devices: 32 us -> 80.6 us  [exchange(): return lax.all_to_all(x, axis, split_axis=0, concat_axis=0, tiled=True)]
    all_to_all x2 -> x3, blocking collectives: 41.2 us -> 71.4 us  [exchange(): return lax.all_to_all(x, axis, split_axis=0, concat_axis=0, tiled=True)]
    all_to_all x4, starting transfers between devices: 52.4 us -> 25.3 us  [exchange(): return lax.all_to_all(x, axis, split_axis=0, concat_axis=0, tiled=True)]
    psum x1 -> x0, blocking collectives: 21.5 us -> none  [on_device(): lax.psum(partial_value.astype(jnp.bfloat16), 'head').astype(jnp.float32)]
    sub x2 -> x0, other arithmetic: 11 us -> none  [attend(): exp_terms = jnp.where(in_range, jnp.exp(scores - row_top), 0.0)]
    reshape x13 -> x14, local copies, waits for them, and re-layouts: 9.84 us -> 7.94 us  [the longest x1 2.51 us: on_device(): moved = moved.reshape(heads_axis * groups * share, wide)]
  transfers between devices with their start and end apart: 8 -> 7, of which waited for: 6 -> 4; matrix products, arithmetic and copies ran while one was open for 11% -> 13% of each run, Pallas kernels for 0% -> 0%
where the time goes in v1:
time: 236 us; the launch traced here: 235 us
  waiting for transfers between devices  80.7 us (34%)
  blocking collectives  71.4 us (30%)
  starting transfers between devices  25.4 us (11%)
  matrix products  19.4 us (8%)
  local copies, waits for them, and re-layouts  16 us (7%)
  between operations  14.4 us (6%)
  other arithmetic  8.13 us (3%)
    all_to_all x4, waiting for transfers between devices, exchange(): return lax.all_to_all(x, axis, split_axis=0, concat_axis=0, tiled=True)  80.6 us
    all_to_all x3, blocking collectives, exchange(): return lax.all_to_all(x, axis, split_axis=0, concat_axis=0, tiled=True)  71.4 us
    all_to_all x4, starting transfers between devices, exchange(): return lax.all_to_all(x, axis, split_axis=0, concat_axis=0, tiled=True)  25.3 us
    dot_general x16, matrix products, dot(): lax.dot_general(a, b, (dims, ((), ())), precision=precision, preferred_el...  7.94 us
    dot_general x2, matrix products, hidden_of(): gate = jnp.dot(x, w_gate[0], preferred_element_type=F32)  4.86 us
  transfers between devices with their start and end apart: 7, of which 4 were waited for; matrix products, arithmetic and copies ran while one was open for 13% of the time, Pallas kernels for 0%

profile of v1, /device:TPU:1, one launch (start us, length us, event | category | flops | bytes accessed | tf_op | source)
XLA Modules:
  0.0 235.3 jit_solution(11181527579368919226)
XLA Ops:
  7.3 0.8 slice_bitcast_fusion.1
  8.2 0.2 compare_reduce_fusion
  8.4 0.1 fusion.24
  8.6 1.0 convolution_convert_fusion.3
  9.7 23.4 %all_to_all.35 = bf16[64,4,512]{2,1,0:T(4,128)(2,1)S(1)} all-to-all(bf16[64,4,512]{2,1,0:T(4,128)(2,1)S(1)} %reshape.292), channel_id=1, replica_groups=mesh['expert'=64,'head'=8] {'expert'}, dimensions={0} | all-to-all | bytes 524288 | tf_op jit(solution)/shard_map/all_to_all | solution.py:25
  33.1 0.8 reshape.297
  33.9 1.3 copy.65
  35.2 10.2 %all-to-all-start.1 = ((bf16[8,128,512]{1,2,0:T(8,128)(2,1)}), bf16[8,128,512]{1,2,0:T(8,128)(2,1)S(1)}, u32[]{:S(2)}, u32[]{:S(2)}) async-start(bf16[8,128,512]{1,2,0:T(8,128)(2,1)} %bitcast.9), calls=%async_computation.1 | async-start | bytes 2097152 | tf_op jit(solution)/shard_map/all_to_all | solution.py:25
  45.5 1.0 constant_dynamic-slice_fusion
  46.5 0.6 fusion.99
  47.4 0.3 convolution_convert_fusion
  47.8 0.1 fusion.23
  47.9 0.3 convolution_convert_fusion.4
  48.3 0.2 copy-done.15
  48.5 1.0 pad_maximum_fusion
  49.5 36.0 %all-to-all-done.1 = bf16[8,128,512]{1,2,0:T(8,128)(2,1)S(1)} async-done(((bf16[8,128,512]{1,2,0:T(8,128)(2,1)}), bf16[8,128,512]{1,2,0:T(8,128)(2,1)S(1)}, u32[]{:S(2)}, u32[]{:S(2)}) %all-to-all-start.1) | async-done | bytes 1048608 | tf_op jit(solution)/shard_map/all_to_all | solution.py:25
  85.4 1.3 copy.67
  86.7 21.9 %all_to_all.36 = bf16[64,4,896]{2,1,0:T(4,128)(2,1)S(1)} all-to-all(bf16[64,4,896]{2,1,0:T(4,128)(2,1)} %pad_maximum_fusion), channel_id=1, replica_groups=mesh['expert'=64,'head'=8] {'expert'}, dimensions={0} | all-to-all | bytes 917504 | tf_op jit(solution)/shard_map/all_to_all | solution.py:25
  108.8 0.8 reshape.295
  109.6 2.4 %fusion.29 = f32[256,128]{1,0:T(8,128)S(1)} fusion(bf16[256,4096]{1,0:T(8,128)(2,1)} %all-gather.8.cloned.1.call-done, bf16[1,4096,128]{2,1,0:T(8,128)(2,1)S(1)} %copy-done.1), kind=kOutput, calls=%fused_computation.42 | convolution fusion | flops 268435456 | bytes 3276800 | tf_op jit(solution)/shard_map/dot_general | solution.py:133
  112.0 0.7 fusion.17
  112.8 0.1 copy.69
  112.9 26.0 %all_to_all.37 = bf16[8,256,128]{1,2,0:T(8,128)(2,1)S(1)} all-to-all(bf16[8,256,128]{1,2,0:T(8,128)(2,1)S(1)} %broadcast_in_dim.99), channel_id=1, replica_groups=mesh['expert'=64,'head'=8] {'head'}, dimensions={0} | all-to-all | bytes 1048576 | tf_op jit(solution)/shard_map/all_to_all | solution.py:25
  138.9 1.7 convolution_convert_fusion.2
  140.6 0.8 reshape.299
  141.4 5.6 %all-to-all-start.4 = ((bf16[64,4,512]{2,1,0:T(4,128)(2,1)}), bf16[64,4,512]{2,1,0:T(4,128)(2,1)S(1)}, u32[]{:S(2)}, u32[]{:S(2)}) async-start(bf16[64,4,512]{2,1,0:T(4,128)(2,1)} %reshape.299), calls=%async_computation.4 | async-start | bytes 524288 | tf_op jit(solution)/shard_map/all_to_all | solution.py:25
  147.2 0.8 fusion.47
  148.1 0.7 reshape.294
  148.8 10.2 %all-to-all-done.4 = bf16[64,4,512]{2,1,0:T(4,128)(2,1)S(1)} async-done(((bf16[64,4,512]{2,1,0:T(4,128)(2,1)}), bf16[64,4,512]{2,1,0:T(4,128)(2,1)S(1)}, u32[]{:S(2)}, u32[]{:S(2)}) %all-to-all-start.4) | async-done | bytes 262176 | tf_op jit(solution)/shard_map/all_to_all | solution.py:25
  159.1 0.2 fusion.20
  159.3 1.3 convolution_convert_fusion.7
  160.7 2.4 %fusion.31 = f32[256,128]{1,0:T(8,128)S(1)} fusion(bf16[256,4096]{1,0:T(8,128)(2,1)} %all-gather.4.cloned.1.call-done, bf16[1,4096,128]{2,1,0:T(8,128)(2,1)S(1)} %copy-done.1), kind=kOutput, calls=%fused_computation.44 | convolution fusion | flops 268435456 | bytes 3276800 | tf_op jit(solution)/shard_map/dot_general | solution.py:133
  163.1 0.7 fusion.16
  163.9 1.0 broadcast_in_dim.100
  164.9 3.5 %all-to-all-start.5 = ((bf16[8,376,128]{2,1,0:T(8,128)(2,1)}), bf16[8,376,128]{2,1,0:T(8,128)(2,1)S(1)}, u32[]{:S(2)}, u32[]{:S(2)}) async-start(bf16[8,376,128]{2,1,0:T(8,128)(2,1)} %broadcast_in_dim.100), calls=%async_computation.5 | async-start | bytes 1540096 | tf_op jit(solution)/shard_map/all_to_all | solution.py:25
  168.5 0.1 fusion.39
  168.6 0.2 broadcast_in_dim.90
  168.8 0.9 reshape.286
  169.7 1.3 fusion.80
  171.0 20.8 %all-to-all-done.5 = bf16[8,376,128]{2,1,0:T(8,128)(2,1)S(1)} async-done(((bf16[8,376,128]{2,1,0:T(8,128)(2,1)}), bf16[8,376,128]{2,1,0:T(8,128)(2,1)S(1)}, u32[]{:S(2)}, u32[]{:S(2)}) %all-to-all-start.5) | async-done | bytes 770080 | tf_op jit(solution)/shard_map/all_to_all | solution.py:25
  191.9 1.0 copy.80
  192.9 2.2 convolution_convert_fusion.1
  195.1 1.1 reshape.302
  196.3 0.1 copy.85
  196.5 0.1 multiply_reduce_fusion
  196.6 0.8 multiply_convert_fusion
  197.4 1.0 convolution_convert_fusion.6
  198.5 0.9 pad_maximum_fusion.1
  199.4 6.0 %all-to-all-start.6 = ((bf16[64,4,768]{2,1,0:T(4,128)(2,1)}), bf16[64,4,768]{2,1,0:T(4,128)(2,1)S(1)}, u32[]{:S(2)}, u32[]{:S(2)}) async-start(bf16[64,4,768]{2,1,0:T(4,128)(2,1)} %pad_maximum_fusion.1), calls=%async_computation.6 | async-start | bytes 786432 | tf_op jit(solution)/shard_map/all_to_all | solution.py:25
  205.4 0.4 fusion.103
  205.9 0.2 fusion.46
  206.1 0.3 fusion.13
  206.5 13.5 %all-to-all-done.6 = bf16[64,4,768]{2,1,0:T(4,128)(2,1)S(1)} async-done(((bf16[64,4,768]{2,1,0:T(4,128)(2,1)}), bf16[64,4,768]{2,1,0:T(4,128)(2,1)S(1)}, u32[]{:S(2)}, u32[]{:S(2)}) %all-to-all-start.6) | async-done | bytes 393248 | tf_op jit(solution)/shard_map/all_to_all | solution.py:25
  220.3 0.2 fusion.22
  220.5 0.6 pad_maximum_fusion.4
  221.1 0.2 convolution_compare_fusion.1
  221.3 1.2 fusion.102
  222.6 2.5 %reshape.296 = bf16[1024,768]{1,0:T(8,128)(2,1)S(1)} reshape(bf16[2048,384]{1,0:T(8,128)(2,1)} %all-gather.6.cloned.1.call-done) | data formatting | bytes 3145728 | tf_op jit(solution)/shard_map/reshape | solution.py:118
  225.1 1.1 convolution_compare_fusion
  226.2 0.7 fusion.101
  227.0 0.3 fusion.33
  227.3 0.4 fusion.25
  227.8 0.2 fusion.14
  228.0 0.8 pad_maximum_fusion.2
  (90 shorter events, 1.9 us)
Async XLA Ops:
  7.2 104.9 %copy-start = (bf16[1,4096,128]{2,1,0:T(8,128)(2,1)S(1)}, bf16[1,4096,128]{2,1,0:T(8,128)(2,1)}, u32[]{:S(2)}) copy-start(bf16[1,4096,128]{2,1,0:T(8,128)(2,1)} %param.22) | copy-start | bytes 3145732
  7.2 26.7 %copy-start.4 = (bf16[1,128,4096]{2,1,0:T(8,128)(2,1)S(1)}, bf16[1,128,4096]{2,1,0:T(8,128)(2,1)}, u32[]{:S(2)}) copy-start(bf16[1,128,4096]{2,1,0:T(8,128)(2,1)} %param.23) | copy-start | bytes 3145732
  7.2 102.4 %all-gather.8.cloned.1.call-start = ((), (), s32[]{:S(2)}) async-start(), calls=%async_computation.9 | async-start | bytes 2359296 | tf_op jit(solution)/shard_map/all_gather | solution.py:90
  33.9 12.6 %copy-start.19 = (s32[1,24]{1,0:T(1,128)S(1)}, s32[1,24]{1,0:T(1,128)}, u32[]{:S(2)}) copy-start(s32[1,24]{1,0:T(1,128)} %param.19) | copy-start | bytes 292
  33.9 13.2 %copy-start.17 = (s32[24]{0:T(128)S(1)}, s32[24]{0:T(128)}, u32[]{:S(2)}) copy-start(s32[24]{0:T(128)} %param.16) | copy-start | bytes 292
  33.9 13.5 %copy-start.18 = (s32[1,24]{1,0:T(1,128)S(1)}, s32[1,24]{1,0:T(1,128)}, u32[]{:S(2)}) copy-start(s32[1,24]{1,0:T(1,128)} %param.20) | copy-start | bytes 292
  35.2 12.7 %copy-start.7 = (bf16[2,24,512]{2,1,0:T(8,128)(2,1)S(1)}, bf16[2,24,512]{2,1,0:T(8,128)(2,1)}, u32[]{:S(2)}) copy-start(bf16[2,24,512]{2,1,0:T(8,128)(2,1)} %param.13) | copy-start | bytes 147460
  35.2 50.2 %all-to-all-start.1 = ((bf16[8,128,512]{1,2,0:T(8,128)(2,1)}), bf16[8,128,512]{1,2,0:T(8,128)(2,1)S(1)}, u32[]{:S(2)}, u32[]{:S(2)}) async-start(bf16[8,128,512]{1,2,0:T(8,128)(2,1)} %bitcast.9), calls=%async_computation.1 | async-start | bytes 2097152 | tf_op jit(solution)/shard_map/all_to_all | solution.py:25
  45.4 115.3 %all-gather.4.cloned.1.call-start = ((), (), s32[]{:S(2)}) async-start(), calls=%async_computation.7 | async-start | bytes 2359296 | tf_op jit(solution)/shard_map/all_gather | solution.py:112
  46.5 0.7 copy-start.12
  47.9 0.6 copy-start.15
  49.5 60.1 %copy-start.1 = (bf16[1,4096,128]{2,1,0:T(8,128)(2,1)S(1)}, bf16[1,4096,128]{2,1,0:T(8,128)(2,1)}, u32[]{:S(2)}) copy-start(bf16[1,4096,128]{2,1,0:T(8,128)(2,1)} %param.21) | copy-start | bytes 3145732
  109.6 2.5 %copy-start.2 = (bf16[256,4096]{1,0:T(8,128)(2,1)S(1)}, bf16[256,4096]{1,0:T(8,128)(2,1)}, u32[]{:S(2)}) copy-start(bf16[256,4096]{1,0:T(8,128)(2,1)} %all-gather.8.cloned.1.call-done) | copy-start | bytes 6291460
  112.9 34.1 %copy-start.14 = (f32[2,24,8]{1,2,0:T(8,128)S(1)}, f32[2,24,8]{1,2,0:T(8,128)}, u32[]{:S(2)}) copy-start(f32[2,24,8]{1,2,0:T(8,128)} %param.18) | copy-start | bytes 4612
  141.4 17.6 %all-to-all-start.4 = ((bf16[64,4,512]{2,1,0:T(4,128)(2,1)}), bf16[64,4,512]{2,1,0:T(4,128)(2,1)S(1)}, u32[]{:S(2)}, u32[]{:S(2)}) async-start(bf16[64,4,512]{2,1,0:T(4,128)(2,1)} %reshape.299), calls=%async_computation.4 | async-start | bytes 524288 | tf_op jit(solution)/shard_map/all_to_all | solution.py:25
  160.7 2.5 %copy-start.3 = (bf16[256,4096]{1,0:T(8,128)(2,1)S(1)}, bf16[256,4096]{1,0:T(8,128)(2,1)}, u32[]{:S(2)}) copy-start(bf16[256,4096]{1,0:T(8,128)(2,1)} %all-gather.4.cloned.1.call-done) | copy-start | bytes 6291460
  164.9 27.0 %all-to-all-start.5 = ((bf16[8,376,128]{2,1,0:T(8,128)(2,1)}), bf16[8,376,128]{2,1,0:T(8,128)(2,1)S(1)}, u32[]{:S(2)}, u32[]{:S(2)}) async-start(bf16[8,376,128]{2,1,0:T(8,128)(2,1)} %broadcast_in_dim.100), calls=%async_computation.5 | async-start | bytes 1540096 | tf_op jit(solution)/shard_map/all_to_all | solution.py:25
  168.5 24.5 %copy-start.5 = (bf16[8,128,512]{2,1,0:T(8,128)(2,1)S(1)}, bf16[8,128,512]{2,1,0:T(8,128)(2,1)}, u32[]{:S(2)}) copy-start(bf16[8,128,512]{2,1,0:T(8,128)(2,1)} %copy.67) | copy-start | bytes 3145732
  168.5 54.1 %all-gather.6.cloned.1.call-start = ((), (), s32[]{:S(2)}) async-start(), calls=%async_computation.8 | async-start | bytes 1769472 | tf_op jit(solution)/shard_map/all_gather | solution.py:117
  195.1 10.3 %copy-start.6 = (bf16[24,16,576]{2,1,0:T(8,128)(2,1)S(1)}, bf16[24,16,576]{2,1,0:T(8,128)(2,1)}, u32[]{:S(2)}) copy-start(bf16[24,16,576]{2,1,0:T(8,128)(2,1)} %param.15) | copy-start | bytes 1327108
  195.1 10.3 %copy-start.9 = (bf16[2,24,8,576]{3,2,1,0:T(8,128)(2,1)S(1)}, bf16[2,24,8,576]{3,2,1,0:T(8,128)(2,1)}, u32[]{:S(2)}) copy-start(bf16[2,24,8,576]{3,2,1,0:T(8,128)(2,1)} %param.14) | copy-start | bytes 1327108
  199.4 20.6 %all-to-all-start.6 = ((bf16[64,4,768]{2,1,0:T(4,128)(2,1)}), bf16[64,4,768]{2,1,0:T(4,128)(2,1)S(1)}, u32[]{:S(2)}, u32[]{:S(2)}) async-start(bf16[64,4,768]{2,1,0:T(4,128)(2,1)} %pad_maximum_fusion.1), calls=%async_computation.6 | async-start | bytes 786432 | tf_op jit(solution)/shard_map/all_to_all | solution.py:25
  205.8 14.4 %copy-start.8 = (bf16[2,24,512]{2,1,0:T(8,128)(2,1)S(1)}, bf16[2,24,512]{2,1,0:T(8,128)(2,1)}, u32[]{:S(2)}) copy-start(bf16[2,24,512]{2,1,0:T(8,128)(2,1)} %param.13) | copy-start | bytes 147460
  205.9 14.4 %copy-start.11 = (f32[24,256]{1,0:T(8,128)S(1)}, f32[24,256]{1,0:T(8,128)}, u32[]{:S(2)}) copy-start(f32[24,256]{1,0:T(8,128)} %get-tuple-element.14) | copy-start | bytes 73732
  205.9 14.4 %copy-start.16 = (pred[24,256]{1,0:T(8,128)(4,1)S(1)}, pred[24,256]{1,0:T(8,128)(4,1)}, u32[]{:S(2)}) copy-start(pred[24,256]{1,0:T(8,128)(4,1)} %copy-done.15) | copy-start | bytes 18436
  205.9 15.3 %copy-start.13 = (bf16[24,192]{1,0:T(8,128)(2,1)S(1)}, bf16[24,192]{1,0:T(8,128)(2,1)}, u32[]{:S(2)}) copy-start(bf16[24,192]{1,0:T(8,128)(2,1)} %copy-done.12) | copy-start | bytes 27652
  222.5 3.7 %copy-start.10 = (bf16[2,24,8,576]{3,2,1,0:T(8,128)(2,1)S(1)}, bf16[2,24,8,576]{3,2,1,0:T(8,128)(2,1)}, u32[]{:S(2)}) copy-start(bf16[2,24,8,576]{3,2,1,0:T(8,128)(2,1)} %param.14) | copy-start | bytes 1327108
Sparse Core Ops, SparseCore 0:
  34.0 59.5 all-gather.7
  109.7 42.9 all-gather.3
  171.4 39.2 all-gather.5

commit v2 on v1

v2 whole, which is shorter than its diff:
```python
import jax
import jax.numpy as jnp
from jax import lax
from jax.experimental import pallas as pl
from jax.experimental.pallas import tpu as pltpu
from jax.sharding import PartitionSpec as P

KVR = 512
TOPK = 8
STEPS = 2
CAP = 4
ROWS = 24
LAT = 576
CACHE = 16
LANES = 128

SCORE_SCALE = 192.0 ** (-0.5)
ROUTE_SCALE = 2.5
NORM_EPS = 1e-06
LOW = -1e30

BF = jnp.bfloat16
F32 = jnp.float32


def dot(a, b, dims, precision=None):
    return lax.dot_general(a, b, (dims, ((), ())), precision=precision, preferred_element_type=F32)


def exchange(x, axis):
    return lax.all_to_all(x, axis, split_axis=0, concat_axis=0, tiled=True)


def together(*arrays):
    return lax.optimization_barrier(arrays)


def places_of(ids, groups, per):
    rows = ids.shape[0]
    column = lax.broadcasted_iota(jnp.int32, (1, 1, groups * per), 2)
    hit = ids[:, :, None] == column // per
    named = jnp.any(hit, axis=1)
    earlier = (
        lax.broadcasted_iota(jnp.int32, (rows, rows), 1)
        < lax.broadcasted_iota(jnp.int32, (rows, rows), 0)
    ).astype(BF)
    before = dot(earlier, named.astype(BF), ((1,), (0,)))
    return named & (before == (column[0] % CAP).astype(F32)), hit


def mix_of(ids, score, groups):
    place, hit = places_of(ids, groups, CAP)
    share = ROUTE_SCALE * score / jnp.sum(score, axis=1, keepdims=True)
    weight = jnp.sum(jnp.where(hit, share[:, :, None], 0.0), axis=1)
    return jnp.where(place, weight, 0.0)


def softmax_values(parts):
    top = parts[0][0].max(axis=1, keepdims=True)
    for scores, _, _ in parts[1:]:
        top = jnp.maximum(top, scores.max(axis=1, keepdims=True))
    terms = [jnp.where(mask, jnp.exp(scores - top), 0.0) for scores, mask, _ in parts]
    total = sum(t.sum(axis=1, keepdims=True) for t in terms)
    total = jnp.where(total > 0, total, 1.0)
    return sum(
        dot((t / total).astype(BF), values, ((1,), (0,)))
        for t, (_, _, values) in zip(terms, parts)
    )


def expert_kernel(x, gate_w, up_w, down_w, out, x_in, wide_w, narrow_w, made, *sems):
    feats, block = gate_w.shape[1:]
    count = out.shape[0]
    rows, span = x_in.shape
    step = feats // 4
    starts = range(0, feats, step)

    def fetch(k, source, target):
        copy = pltpu.make_async_copy(source, target, sems[k])
        copy.start()
        return copy

    lots, gates, ups = [], [], []
    for c, at in enumerate(starts):
        part = pl.ds(at, step)
        if at < span:
            lots.append(fetch(c, x.at[:, part], x_in.at[:, part]))
        gates.append(fetch(4 + c, gate_w.at[0, part], wide_w.at[part, pl.ds(0, block)]))
        ups.append(fetch(8 + c, up_w.at[0, part], wide_w.at[part, pl.ds(block, block)]))
    narrow = fetch(12, down_w.at[0], narrow_w)
    sums = [0.0] * (feats // span)
    for c, at in enumerate(starts):
        if at < span:
            lots[c].wait()
        gates[c].wait()
        ups[c].wait()
        lanes = at % span
        sums[at // span] += jnp.dot(
            x_in[:, lanes : lanes + step], wide_w[at : at + step], preferred_element_type=F32
        )
    total = sums[0]
    if len(sums) == 2:
        total = total + jnp.concatenate([sums[1][CAP:], sums[1][:CAP]], axis=0)
    hidden = (jax.nn.silu(total[:, :block]) * total[:, block:]).astype(BF)
    if len(sums) == 2:
        line = lax.broadcasted_iota(jnp.int32, (count, rows), 0)
        column = lax.broadcasted_iota(jnp.int32, (count, rows), 1)
        keep = (line + line // CAP * CAP == column).astype(BF)
        hidden = jnp.dot(keep, hidden, preferred_element_type=F32).astype(BF)
    narrow.wait()
    sent = []
    for c, at in enumerate(starts):
        made[:, at : at + step] = jnp.dot(
            hidden, narrow_w[:, at : at + step], preferred_element_type=F32
        ).astype(BF)
        part = pl.ds(at, step)
        sent.append(fetch(13 + c, made.at[:, part], out.at[:, part]))
    for copy in sent:
        copy.wait()


def expert_part(x, span, count, w_gate, w_up, w_down, *waits):
    feats, block = w_gate.shape[1:]

    def kernel(*refs):
        refs = refs[:4] + refs[4 + len(waits) :]
        expert_kernel(*refs)

    return pl.pallas_call(
        kernel,
        out_shape=jax.ShapeDtypeStruct((count, feats), BF),
        in_specs=[pl.BlockSpec(memory_space=pltpu.HBM)] * (4 + len(waits)),
        out_specs=pl.BlockSpec(memory_space=pltpu.HBM),
        scratch_shapes=[
            pltpu.VMEM((x.shape[0], span), BF),
            pltpu.VMEM((feats, 2 * block), BF),
            pltpu.VMEM((block, feats), BF),
            pltpu.VMEM((count, feats), BF),
        ]
        + [pltpu.SemaphoreType.DMA] * 17,
        compiler_params=pltpu.CompilerParams(vmem_limit_bytes=60 * 2**20),
        cost_estimate=pl.CostEstimate(
            flops=6 * count * feats * block,
            bytes_accessed=4 * count * feats + 6 * feats * block,
            transcendentals=count * block,
        ),
    )(x, w_gate, w_up, w_down, *waits)


def pack_kernel(places, tokens, targets, tiles, out):
    feats = tokens.shape[2]
    half = tokens.shape[0] // 2
    for c in range(half):
        lines = sum(
            jnp.dot(places[h], tokens[h * half + c], preferred_element_type=F32) for h in range(2)
        )
        out[:, c * feats : (c + 1) * feats] = lines.astype(BF)
    out[:, half * feats :] = jnp.dot(
        targets[...], tiles[...], preferred_element_type=F32
    ).astype(BF)


def collect_kernel(x, out):
    lines = x.shape[0]
    own = (
        lax.broadcasted_iota(jnp.int32, (ROWS, LANES), 1)
        == lax.broadcasted_iota(jnp.int32, (ROWS, LANES), 0) + (LAT - KVR)
    ).astype(BF)
    marked = (dot(own, x[:, LANES:], ((1,), (1,))) > 0.5).astype(BF)
    block = (
        lax.broadcasted_iota(jnp.int32, (lines, lines), 0) // 8
        == lax.broadcasted_iota(jnp.int32, (lines, lines), 1) // 8
    ).astype(BF)
    chosen = dot(marked, block, ((1,), (0,)))
    place = lax.broadcasted_iota(jnp.int32, (ROWS, lines), 1) % 8
    picks = [jnp.where((place == q) & (chosen > 0.5), 1.0, 0.0).astype(BF) for q in range(8)]
    found = [dot(pick, x[:, :LANES], ((1,), (0,))) for pick in picks]
    found += [dot(pick, x[:, LANES:], ((1,), (0,))) for pick in picks[: CACHE // 8]]
    out[...] = jnp.concatenate(found, axis=0).astype(BF)


def attend_kernel(earlier, query, fresh, *refs):
    caches, out = refs[:-1], refs[-1]
    out[0] = earlier[...]
    rows, wide = query.shape
    lanes = wide - KVR
    slot = lax.broadcasted_iota(jnp.int32, (rows, lanes), 0) // (rows // ROWS)
    lane = lax.broadcasted_iota(jnp.int32, (rows, lanes), 1)
    own = (lane == slot + (LAT - KVR)).astype(BF)
    tiles = KVR // lanes
    held = [x[...] for x in caches] if len(caches) > 1 else [caches[0][h] for h in range(8)]
    share = held[0].shape[0] // ROWS // (tiles + 1)
    values, rests = [], []
    for x in held:
        x = [x[at : at + ROWS] for at in range(0, x.shape[0], ROWS)]
        for p in range(share):
            values.append(jnp.concatenate(x[p * tiles : (p + 1) * tiles], axis=1))
            rests.append(x[share * tiles + p])
    old = jnp.concatenate(
        [jnp.concatenate(values, axis=0), jnp.concatenate(rests, axis=0)], axis=1
    )
    parts = []
    for keys in (old, fresh[...]):
        scores = dot(query[...], keys, ((1,), (1,))) * SCORE_SCALE
        mask = dot(own, keys[:, KVR:], ((1,), (1,))) > 0.5
        parts.append((jnp.where(mask, scores, LOW), mask, keys[:, :KVR]))
    out[1] = softmax_values(parts).astype(BF)


def on_device(
    tokens,
    queries,
    latent_cache,
    lengths,
    expert_ids,
    route_score,
    survive,
    destination,
    w_gate,
    w_up,
    w_down,
    w_latent,
    kv_gain,
):
    groups = lax.axis_size("expert")
    heads_axis = lax.axis_size("head")
    rows, positions, width = latent_cache.shape
    heads = queries.shape[2]
    feats = tokens.shape[2]
    wide = 640

    place, _ = places_of(expert_ids[0], groups, CAP)
    sending = dot(place.astype(BF), tokens[0], ((0,), (0,))).astype(BF)
    arrived0 = exchange(sending.reshape(groups, CAP, feats), "expert")
    rows0 = lax.all_gather(arrived0.reshape(groups * CAP, feats), "head", axis=1, tiled=True)

    def everywhere(x):
        return exchange(jnp.broadcast_to(x[None], (heads_axis,) + x.shape), "head")

    alive = survive[0] == 1
    eye = jnp.eye(rows, LANES - (width - KVR), dtype=BF)
    target = (destination[0][:, None] == jnp.arange(groups)[None, :]).astype(BF)
    share = positions // heads_axis
    tiles = KVR // LANES
    per = share * tiles
    first = lax.axis_index("head") * share
    held = lax.dynamic_slice_in_dim(latent_cache, first, share, axis=1)
    spot = first + lax.broadcasted_iota(jnp.int32, (rows, share), 1)
    valid = ((spot < lengths[:, None]) & alive[:, None]).astype(BF)
    rest = jnp.concatenate([held[:, :, KVR:], valid[:, :, None] * eye[:, None, :]], axis=2)
    rest = jnp.pad(rest, ((0, 0), (0, per - share), (0, 0)))
    cache_tiles = jnp.concatenate([held[:, :, :KVR].reshape(rows, per, LANES), rest], axis=2)
    cache_tiles = cache_tiles.transpose(1, 0, 2).reshape(per * rows, 2 * LANES)

    column = lax.broadcasted_iota(jnp.int32, (1, groups * per), 1)
    place8, _ = places_of(expert_ids[1], groups, per)
    places = jnp.stack(
        [jnp.where(column % per // CAP == h, place8, False).astype(BF).T for h in range(2)]
    )
    to = destination[0][:, None] == column // per
    targets = jnp.stack([to & (column % per == q) for q in range(per)])
    targets = targets.reshape(per * rows, groups * per).astype(BF).T

    own, arrived0, places, targets, cache_tiles = together(
        tokens[1], arrived0, places, targets, cache_tiles
    )
    both = pl.pallas_call(
        pack_kernel,
        out_shape=jax.ShapeDtypeStruct(
            (groups * per, heads_axis * feats // 2 + 2 * LANES), BF
        ),
        in_specs=[pl.BlockSpec(memory_space=pltpu.VMEM)] * 4,
        out_specs=pl.BlockSpec(memory_space=pltpu.VMEM),
        compiler_params=pltpu.CompilerParams(vmem_limit_bytes=32 * 2**20),
    )(places, everywhere(own), targets, cache_tiles)
    both = exchange(both.reshape(groups, per, both.shape[1]), "expert")
    both = both.reshape(groups * per, both.shape[2])

    parts0 = expert_part(rows0, heads_axis * feats, groups * CAP, w_gate, w_up, w_down)
    parts1 = expert_part(
        both, heads_axis * feats // 2, groups * CAP, w_gate, w_up, w_down, parts0
    )

    pieces = both[:, heads_axis * feats // 2 :]
    pieces, parts1 = together(pieces, parts1)
    pieces = pl.pallas_call(
        collect_kernel,
        out_shape=jax.ShapeDtypeStruct(((per + share) * rows, LANES), BF),
        in_specs=[pl.BlockSpec(memory_space=pltpu.VMEM)],
        out_specs=pl.BlockSpec(memory_space=pltpu.VMEM),
    )(pieces)
    right = [(i, (i + 1) % heads_axis) for i in range(heads_axis)]
    left = [(i, (i - 1) % heads_axis) for i in range(heads_axis)]
    ahead, behind = [pieces], [pieces]
    for step in range(heads_axis // 4):
        ahead.append(lax.ppermute(ahead[-1], "head", right))
        behind.append(lax.ppermute(behind[-1], "head", left))

    q0 = queries[0].reshape(rows * heads, width)
    keys0 = latent_cache.reshape(rows * positions, width)
    row_of = lax.broadcasted_iota(jnp.int32, (rows, 1, rows, positions), 0)
    key_of = lax.broadcasted_iota(jnp.int32, (rows, 1, rows, positions), 2)
    spot = lax.broadcasted_iota(jnp.int32, (rows, 1, rows, positions), 3)
    mask0 = (row_of == key_of) & (spot < lengths[:, None, None, None])
    mask0 = jnp.broadcast_to(mask0, (rows, heads, rows, positions)).reshape(
        rows * heads, rows * positions
    )
    scores0 = jnp.where(mask0, dot(q0, keys0, ((1,), (1,))) * SCORE_SCALE, LOW)
    attn0 = softmax_values([(scores0, mask0, keys0[:, :KVR])]).astype(BF)

    def answers_of(parts):
        summed = lax.psum_scatter(parts, "head", scatter_dimension=1, tiled=True)
        return summed.reshape(groups, CAP, feats)

    def combine(s, back):
        back = back.reshape(groups * CAP, feats).astype(F32)
        mixed = dot(mix_of(expert_ids[s], route_score[s], groups), back, ((1,), (0,)), precision=lax.Precision.HIGHEST)
        return (tokens[s].astype(F32) + mixed).astype(BF)

    answers0 = answers_of(parts0)
    answers1 = answers_of(parts1)
    layer0 = combine(0, exchange(answers0, "expert"))

    part = jnp.dot(layer0, w_latent, preferred_element_type=F32).astype(BF)
    part, ahead[-1], behind[-1] = together(part, ahead[-1], behind[-1])
    for step in range(heads_axis // 4):
        ahead.append(lax.ppermute(ahead[-1], "head", right))
        if step + 1 < heads_axis // 4:
            behind.append(lax.ppermute(behind[-1], "head", left))
    whole_sum = everywhere(part).astype(F32).sum(axis=0)
    leading = whole_sum[:, :KVR]
    norm = lax.rsqrt(jnp.mean(leading * leading, axis=1, keepdims=True) + NORM_EPS)
    latent = jnp.concatenate(
        [
            (leading * norm * kv_gain).astype(BF),
            whole_sum[:, KVR:width].astype(BF),
            alive.astype(BF)[:, None] * eye,
        ],
        axis=1,
    )
    sent = dot(target, jnp.pad(latent, ((0, 0), (0, 1024 - wide))), ((0,), (0,))).astype(BF)
    answers1, ahead[-2], behind[-1] = together(answers1, ahead[-2], behind[-1])
    caches = ahead + behind[1:]
    last = exchange(
        jnp.concatenate([answers1, sent.reshape(groups, CAP, 1024 // CAP)], axis=2), "expert"
    )
    layer1 = combine(1, last[:, :, :feats])
    fresh = last[:, :, feats:].reshape(groups, 1024)[:, :wide]

    q1 = jnp.pad(queries[1].reshape(rows * heads, width), ((0, 0), (0, wide - width)))
    attn = pl.pallas_call(
        attend_kernel,
        out_shape=jax.ShapeDtypeStruct((STEPS, rows * heads, KVR), BF),
        in_specs=[pl.BlockSpec(memory_space=pltpu.VMEM)] * (3 + len(caches)),
        out_specs=pl.BlockSpec(memory_space=pltpu.VMEM),
        compiler_params=pltpu.CompilerParams(vmem_limit_bytes=32 * 2**20),
    )(attn0, q1, fresh, *caches)
    return attn.reshape(STEPS, rows, heads, KVR), jnp.stack([layer0, layer1])


def solution(mesh):
    return jax.shard_map(
        on_device,
        mesh=mesh,
        in_specs=(
            P(None, "expert", "head"),
            P(None, "expert", "head", None),
            P("expert", None, None),
            P("expert"),
            P(None, "expert", None),
            P(None, "expert", None),
            P(None, "expert"),
            P(None, "expert"),
            P("expert", None, "head"),
            P("expert", None, "head"),
            P("expert", "head", None),
            P("head", None),
            P(),
        ),
        out_specs=(P(None, "expert", "head", None), P(None, "expert", "head")),
        check_vma=False,
    )
```

time: 236 us -> 218 us (0.924)
  blocking collectives: 71.4 us -> 19.2 us
  starting transfers between devices: 25.4 us -> 66.5 us
  Pallas kernels: 0 us -> 18.4 us
  matrix products: 19.4 us -> 3.14 us
  local copies, waits for them, and re-layouts: 16 us -> 10.4 us
  waiting for transfers between devices: 80.7 us -> 77.6 us
    all_to_all x3 -> x1, blocking collectives: 71.4 us -> 19.2 us  [exchange(): return lax.all_to_all(x, axis, split_axis=0, concat_axis=0, tiled=True)]
    ppermute x0 -> x7, starting transfers between devices: none -> 21.6 us  [the longest x3 12.5 us: on_device(): behind.append(lax.ppermute(behind[-1], 'head', left))]
    all_to_all x4 -> x5, starting transfers between devices: 25.3 us -> 44.8 us  [exchange(): return lax.all_to_all(x, axis, split_axis=0, concat_axis=0, tiled=True)]
    pallas_call x0 -> x5, Pallas kernels: none -> 18.4 us  [the longest x2 11.8 us: expert_part(): pl.pallas_call(kernel, out_shape=jax.ShapeDtypeStruct((count, feats), BF)...]
    all_to_all x4 -> x5, waiting for transfers between devices: 80.6 us -> 65.7 us  [exchange(): return lax.all_to_all(x, axis, split_axis=0, concat_axis=0, tiled=True)]
    all_gather x1, waiting for transfers between devices: 0.02 us -> 10.8 us  [on_device(): lax.all_gather(arrived0.reshape(groups * CAP, feats), 'head', axis=1, til...]
    dot_general x6 -> x0, matrix products: 10.2 us -> none  [the longest x2 4.86 us: hidden_of(): gate = jnp.dot(x, w_gate[0], preferred_element_type=F32)]
    dot_general x16 -> x9, matrix products: 7.94 us -> 2.88 us  [dot(): lax.dot_general(a, b, (dims, ((), ())), precision=precision, preferred_el...]
  transfers between devices with their start and end apart: 7 -> 15, of which waited for: 4 -> 8; matrix products, arithmetic and copies ran while one was open for 13% -> 7% of each run, Pallas kernels for 0% -> 8%
where the time goes in v2:
time: 218 us; the launch traced here: 217 us
  waiting for transfers between devices  77.6 us (36%)
  starting transfers between devices  66.5 us (31%)
  blocking collectives  19.2 us (9%)
  Pallas kernels  18.4 us (8%)
  between operations  14.4 us (7%)
  local copies, waits for them, and re-layouts  10.4 us (5%)
  other arithmetic  7.24 us (3%)
  matrix products  3.14 us (1%)
    all_to_all x5, waiting for transfers between devices, exchange(): return lax.all_to_all(x, axis, split_axis=0, concat_axis=0, tiled=True)  65.7 us
    all_to_all x5, starting transfers between devices, exchange(): return lax.all_to_all(x, axis, split_axis=0, concat_axis=0, tiled=True)  44.8 us
    all_to_all x1, blocking collectives, exchange(): return lax.all_to_all(x, axis, split_axis=0, concat_axis=0, tiled=True)  19.2 us
    ppermute x3, starting transfers between devices, on_device(): behind.append(lax.ppermute(behind[-1], 'head', left))  12.5 us
    pallas_call x2, Pallas kernels, expert_part(): pl.pallas_call(kernel, out_shape=jax.ShapeDtypeStruct((count, feats), BF)...  11.8 us
    all_gather x1, waiting for transfers between devices, on_device(): lax.all_gather(arrived0.reshape(groups * CAP, feats), 'head', axis=1, til...  10.8 us
    ppermute x4, starting transfers between devices, on_device(): ahead.append(lax.ppermute(ahead[-1], 'head', right))  9.11 us
  transfers between devices with their start and end apart: 15, of which 8 were waited for; matrix products, arithmetic and copies ran while one was open for 7% of the time, Pallas kernels for 8%

profile of v2, /device:TPU:1, one launch (start us, length us, event | category | flops | bytes accessed | tf_op | source)
XLA Modules:
  0.0 216.9 jit_solution(16149902081700974204)
XLA Ops:
  7.2 0.8 slice_bitcast_fusion.3
  8.2 0.2 compare_reduce_fusion.1
  8.4 0.1 fusion.5
  8.5 1.0 convolution_convert_fusion
  9.5 0.8 reshape.976
  10.3 11.6 %all-to-all-start = ((bf16[64,4,512]{2,1,0:T(4,128)(2,1)}), bf16[64,4,512]{2,1,0:T(4,128)(2,1)S(1)}, u32[]{:S(2)}, u32[]{:S(2)}) async-start(bf16[64,4,512]{2,1,0:T(4,128)(2,1)} %reshape.976), calls=%async_computation | async-start | bytes 524288 | tf_op jit(solution)/shard_map/all_to_all | solution.py:31
  22.1 0.7 fusion.33
  22.8 0.7 fusion.34
  23.5 0.7 fusion.35
  24.3 0.7 fusion.36
  25.0 0.7 fusion.37
  25.8 8.2 %all-to-all-done = bf16[64,4,512]{2,1,0:T(4,128)(2,1)S(1)} async-done(((bf16[64,4,512]{2,1,0:T(4,128)(2,1)}), bf16[64,4,512]{2,1,0:T(4,128)(2,1)S(1)}, u32[]{:S(2)}, u32[]{:S(2)}) %all-to-all-start) | async-done | bytes 262176 | tf_op jit(solution)/shard_map/all_to_all | solution.py:31
  33.9 0.8 reshape.981
  35.1 0.1 copy.49
  35.3 0.1 copy.50
  35.5 0.1 broadcast_multiply_fusion
  35.8 0.2 compare_reduce_fusion
  36.0 0.1 select_bitcast_fusion.1
  36.2 0.3 copy.48
  36.6 19.2 %all_to_all.30.tokens = bf16[8,24,512]{2,1,0:T(8,128)(2,1)S(1)} all-to-all(bf16[8,24,512]{2,1,0:T(8,128)(2,1)S(1)} %broadcast_in_dim.91), channel_id=1, replica_groups=mesh['expert'=64,'head'=8] {'head'}, dimensions={0} | all-to-all | bytes 393216 | tf_op jit(solution)/shard_map/all_to_all | solution.py:31
  55.8 2.7 %shard_map.143 = bf16[512,2304]{1,0:T(8,128)(2,1)} custom-call(bf16[2,512,24]{2,1,0:T(8,128)(2,1)S(1)} %stack.37.places, bf16[8,24,512]{2,1,0:T(8,128)(2,1)S(1)} %all_to_all.30.tokens, bf16[512,192]{1,0:T(8,128)(2,1)S(1)} %bitcast.62, bf16[192,256]{1,0:T(8,128)(2,1)S(1)} %bitcast.63), custom_call_target="tpu_custom_call" | custom-call | tf_op jit(solution)/shard_map/pallas_call | solution.py:267
  58.5 8.0 %all-to-all-start.2 = ((bf16[64,8,2304]{2,1,0:T(8,128)(2,1)}), bf16[64,8,2304]{2,1,0:T(8,128)(2,1)S(1)}, u32[]{:S(2)}, u32[]{:S(2)}) async-start(bf16[64,8,2304]{2,1,0:T(8,128)(2,1)} %bitcast.16), calls=%async_computation.2 | async-start | bytes 4718592 | tf_op jit(solution)/shard_map/all_to_all | solution.py:31
  66.6 10.8 %all-gather.2.cloned.1.call-done.refs_0_ = bf16[256,4096]{1,0:T(8,128)(2,1)} async-done(((bf16[256,512]{1,0:T(8,128)(2,1)}), bf16[256,4096]{1,0:T(8,128)(2,1)}) %all-gather.2.cloned.1.call-update) | async-done | bytes 2097168 | tf_op jit(solution)/shard_map/all_gather | solution.py:235
  77.3 5.1 %shard_map.144.refs_4_ = bf16[256,4096]{1,0:T(8,128)(2,1)} custom-call(bf16[256,4096]{1,0:T(8,128)(2,1)} %all-gather.2.cloned.1.call-done.refs_0_, bf16[1,4096,128]{2,1,0:T(8,128)(2,1)} %refs_1_.3, bf16[1,4096,128]{2,1,0:T(8,128)(2,1)} %refs_2_.3, bf16[1,128,4096]{2,1,0:T(8,128)(2,1)} %refs_3_.3), custom_call_target="tpu_custom_call" | custom-call | flops 805306368 | bytes 7340032 | tf_op jit(solution)/shard_map/pallas_call | solution.py:129
  82.5 40.6 %all-to-all-done.2 = bf16[64,8,2304]{2,1,0:T(8,128)(2,1)S(1)} async-done(((bf16[64,8,2304]{2,1,0:T(8,128)(2,1)}), bf16[64,8,2304]{2,1,0:T(8,128)(2,1)S(1)}, u32[]{:S(2)}, u32[]{:S(2)}) %all-to-all-start.2) | async-done | bytes 2359328 | tf_op jit(solution)/shard_map/all_to_all | solution.py:31
  123.2 0.8 slice.74.x
  123.9 0.7 copy-done.2
  124.7 6.7 %shard_map.145 = bf16[256,4096]{1,0:T(8,128)(2,1)} custom-call(bf16[512,2304]{1,0:T(8,128)(2,1)} %bitcast.65, bf16[1,4096,128]{2,1,0:T(8,128)(2,1)} %refs_1_.3, bf16[1,4096,128]{2,1,0:T(8,128)(2,1)} %refs_2_.3, bf16[1,128,4096]{2,1,0:T(8,128)(2,1)} %refs_3_.3, bf16[256,4096]{1,0:T(8,128)(2,1)} %shard_map.144.refs_4_), custom_call_target="tpu_custom_call" | custom-call | flops 805306368 | bytes 7340032 | tf_op jit(solution)/shard_map/pallas_call | solution.py:129
  131.4 0.7 copy-done.7
  132.2 1.7 reshape.983
  134.0 6.8 %all-to-all-start.3 = ((bf16[64,4,512]{2,1,0:T(4,128)(2,1)}), bf16[64,4,512]{2,1,0:T(4,128)(2,1)S(1)}, u32[]{:S(2)}, u32[]{:S(2)}) async-start(bf16[64,4,512]{2,1,0:T(4,128)(2,1)} %reshape.983), calls=%async_computation.5 | async-start | bytes 524288 | tf_op jit(solution)/shard_map/all_to_all | solution.py:31
  140.8 0.1 fusion.9
  140.9 2.2 shard_map.146.refs_0_
  143.1 1.9 collective-permute-start
  145.0 4.8 %collective-permute-start.2 = (bf16[240,128]{1,0:T(8,128)(2,1)}, bf16[240,128]{1,0:T(8,128)(2,1)S(1)}, u32[]{:S(2)}, u32[]{:S(2)}) collective-permute-start(bf16[240,128]{1,0:T(8,128)(2,1)} %shard_map.146.refs_0_), channel_id=1, source_target_pairs={{0,7},{1,0},{2,1},{3,2},{4,3},{5,4},{6,5},{7,6},{8,15},{9,8},{10,9... | collective-permute-start | bytes 184328 | tf_op jit(solution)/shard_map/ppermute | solution.py:297
  149.8 0.2 fusion.14
  150.0 0.2 broadcast_in_dim.84
  150.1 0.9 reshape.974
  151.1 0.1 collective-permute-done.refs_1_
  151.2 1.9 collective-permute-start.1
  153.1 4.6 %collective-permute-start.3 = (bf16[240,128]{1,0:T(8,128)(2,1)S(1)}, bf16[240,128]{1,0:T(8,128)(2,1)S(1)}, u32[]{:S(2)}, u32[]{:S(2)}) collective-permute-start(bf16[240,128]{1,0:T(8,128)(2,1)S(1)} %collective-permute-done.2.refs_5_), channel_id=1, source_target_pairs={{0,7},{1,0},{2,1},{3,2},{4,3},{5,4},{6,5},{7,6},{8,15},{9,8},{10,9... | collective-permute-start | bytes 184328 | tf_op jit(solution)/shard_map/ppermute | solution.py:297
  157.8 0.2 fusion.1
  158.0 0.3 convolution_convert_fusion.3
  158.3 0.2 collective-permute-done.1.refs_2_
  158.5 0.7 collective-permute-done.3.refs_6_
  159.3 0.7 broadcast_in_dim.95
  160.0 5.1 %all-to-all-start.4 = ((bf16[8,24,576]{2,1,0:T(8,128)(2,1)}), bf16[8,24,576]{2,1,0:T(8,128)(2,1)S(1)}, u32[]{:S(2)}, u32[]{:S(2)}) async-start(bf16[8,24,576]{2,1,0:T(8,128)(2,1)} %broadcast_in_dim.95), calls=%async_computation.6 | async-start | bytes 491520 | tf_op jit(solution)/shard_map/all_to_all | solution.py:31
  165.1 0.4 fusion.78
  165.6 3.4 %collective-permute-start.4 = (bf16[240,128]{1,0:T(8,128)(2,1)S(1)}, bf16[240,128]{1,0:T(8,128)(2,1)S(1)}, u32[]{:S(2)}, u32[]{:S(2)}) collective-permute-start(bf16[240,128]{1,0:T(8,128)(2,1)S(1)} %collective-permute-done.1.refs_2_), channel_id=1, source_target_pairs={{0,1},{1,2},{2,3},{3,4},{4,5},{5,6},{6,7},{7,0},{8,9},{9,10},{10,1... | collective-permute-start | bytes 184328 | tf_op jit(solution)/shard_map/ppermute | solution.py:327
  168.9 3.1 %collective-permute-start.5 = (bf16[240,128]{1,0:T(8,128)(2,1)S(1)}, bf16[240,128]{1,0:T(8,128)(2,1)S(1)}, u32[]{:S(2)}, u32[]{:S(2)}) collective-permute-start(bf16[240,128]{1,0:T(8,128)(2,1)S(1)} %collective-permute-done.3.refs_6_), channel_id=1, source_target_pairs={{0,7},{1,0},{2,1},{3,2},{4,3},{5,4},{6,5},{7,6},{8,15},{9,8},{10,9... | collective-permute-start | bytes 184328 | tf_op jit(solution)/shard_map/ppermute | solution.py:329
  172.1 4.9 %all-to-all-done.4 = bf16[8,24,576]{2,1,0:T(8,128)(2,1)S(1)} async-done(((bf16[8,24,576]{2,1,0:T(8,128)(2,1)}), bf16[8,24,576]{2,1,0:T(8,128)(2,1)S(1)}, u32[]{:S(2)}, u32[]{:S(2)}) %all-to-all-start.4) | async-done | bytes 221216 | tf_op jit(solution)/shard_map/all_to_all | solution.py:31
  177.1 0.1 multiply_reduce_fusion
  177.3 0.3 convolution_convert_fusion.2
  177.7 1.0 reshape.982
  178.8 0.9 pad_maximum_fusion
  179.7 13.3 %all-to-all-start.5 = ((bf16[64,4,768]{2,1,0:T(4,128)(2,1)}), bf16[64,4,768]{2,1,0:T(4,128)(2,1)S(1)}, u32[]{:S(2)}, u32[]{:S(2)}) async-start(bf16[64,4,768]{2,1,0:T(4,128)(2,1)} %pad_maximum_fusion), calls=%async_computation.7 | async-start | bytes 786432 | tf_op jit(solution)/shard_map/all_to_all | solution.py:31
  193.0 0.2 fusion.12
  193.2 0.1 fusion.7
  193.4 0.3 convolution_convert_fusion.1.earlier
  193.7 1.9 collective-permute-start.6
  195.6 12.0 %all-to-all-done.5 = bf16[64,4,768]{2,1,0:T(4,128)(2,1)S(1)} async-done(((bf16[64,4,768]{2,1,0:T(4,128)(2,1)}), bf16[64,4,768]{2,1,0:T(4,128)(2,1)S(1)}, u32[]{:S(2)}, u32[]{:S(2)}) %all-to-all-start.5) | async-done | bytes 393248 | tf_op jit(solution)/shard_map/all_to_all | solution.py:31
  207.9 0.2 fusion.3
  208.1 0.6 pad_maximum_fusion.1
  208.7 1.7 shard_map.147
  (84 shorter events, 2.0 us)
Async XLA Ops:
  7.2 150.9 %copy-start = (bf16[512,576]{0,1:T(8,128)(2,1)S(1)}, bf16[512,576]{0,1:T(8,128)(2,1)}, u32[]{:S(2)}) copy-start(bf16[512,576]{0,1:T(8,128)(2,1)} %param.24) | copy-start | bytes 1769476
  7.2 27.6 %copy-start.6 = (s32[1,24]{1,0:T(1,128)S(1)}, s32[1,24]{1,0:T(1,128)}, u32[]{:S(2)}) copy-start(s32[1,24]{1,0:T(1,128)} %param.20) | copy-start | bytes 292
  7.2 28.0 %copy-start.10 = (s32[1,24]{1,0:T(1,128)S(1)}, s32[1,24]{1,0:T(1,128)}, u32[]{:S(2)}) copy-start(s32[1,24]{1,0:T(1,128)} %param.19) | copy-start | bytes 292
  7.2 28.0 %copy-start.8 = (s32[24]{0:T(128)S(1)}, s32[24]{0:T(128)}, u32[]{:S(2)}) copy-start(s32[24]{0:T(128)} %param.16) | copy-start | bytes 292
  7.2 28.2 %copy-start.3 = (bf16[24,16,576]{2,1,0:T(8,128)(2,1)S(1)}, bf16[24,16,576]{2,1,0:T(8,128)(2,1)}, u32[]{:S(2)}) copy-start(bf16[24,16,576]{2,1,0:T(8,128)(2,1)} %param.15) | copy-start | bytes 1327108
  9.5 27.0 %copy-start.5 = (bf16[2,24,512]{2,1,0:T(8,128)(2,1)S(1)}, bf16[2,24,512]{2,1,0:T(8,128)(2,1)}, u32[]{:S(2)}) copy-start(bf16[2,24,512]{2,1,0:T(8,128)(2,1)} %param.13) | copy-start | bytes 147460
  10.3 23.6 %all-to-all-start = ((bf16[64,4,512]{2,1,0:T(4,128)(2,1)}), bf16[64,4,512]{2,1,0:T(4,128)(2,1)S(1)}, u32[]{:S(2)}, u32[]{:S(2)}) async-start(bf16[64,4,512]{2,1,0:T(4,128)(2,1)} %reshape.976), calls=%async_computation | async-start | bytes 524288 | tf_op jit(solution)/shard_map/all_to_all | solution.py:31
  21.9 55.4 %all-gather.2.cloned.1.call-start = ((), (), s32[]{:S(2)}) async-start(), calls=%async_computation.8 | async-start | bytes 2359296 | tf_op jit(solution)/shard_map/all_gather | solution.py:235
  58.5 64.6 %all-to-all-start.2 = ((bf16[64,8,2304]{2,1,0:T(8,128)(2,1)}), bf16[64,8,2304]{2,1,0:T(8,128)(2,1)S(1)}, u32[]{:S(2)}, u32[]{:S(2)}) async-start(bf16[64,8,2304]{2,1,0:T(8,128)(2,1)} %bitcast.16), calls=%async_computation.2 | async-start | bytes 4718592 | tf_op jit(solution)/shard_map/all_to_all | solution.py:31
  66.5 65.7 %reduce-scatter.5.cloned.1.call-start = ((), (), s32[]{:S(2)}) async-start(), calls=%async_computation.10 | async-start | bytes 2359296 | tf_op jit(solution)/shard_map/reduce_scatter | solution.py:312
  82.5 95.2 %reduce-scatter.3.cloned.1.call-start = ((), (), s32[]{:S(2)}) async-start(), calls=%async_computation.9 | async-start | bytes 2359296 | tf_op jit(solution)/shard_map/reduce_scatter | solution.py:312
  123.2 1.5 copy-start.2
  131.4 0.7 copy-start.7
  131.4 9.5 %copy-start.4 = (bf16[2,24,8,576]{3,2,1,0:T(8,128)(2,1)S(1)}, bf16[2,24,8,576]{3,2,1,0:T(8,128)(2,1)}, u32[]{:S(2)}) copy-start(bf16[2,24,8,576]{3,2,1,0:T(8,128)(2,1)} %param.14) | copy-start | bytes 1327108
  134.0 23.8 %all-to-all-start.3 = ((bf16[64,4,512]{2,1,0:T(4,128)(2,1)}), bf16[64,4,512]{2,1,0:T(4,128)(2,1)S(1)}, u32[]{:S(2)}, u32[]{:S(2)}) async-start(bf16[64,4,512]{2,1,0:T(4,128)(2,1)} %reshape.983), calls=%async_computation.5 | async-start | bytes 524288 | tf_op jit(solution)/shard_map/all_to_all | solution.py:31
  143.1 8.1 %collective-permute-start = (bf16[240,128]{1,0:T(8,128)(2,1)}, bf16[240,128]{1,0:T(8,128)(2,1)S(1)}, u32[]{:S(2)}, u32[]{:S(2)}) collective-permute-start(bf16[240,128]{1,0:T(8,128)(2,1)} %shard_map.146.refs_0_), channel_id=1, source_target_pairs={{0,1},{1,2},{2,3},{3,4},{4,5},{5,6},{6,7},{7,0},{8,9},{9,10},{10,1... | collective-permute-start | bytes 184328 | tf_op jit(solution)/shard_map/ppermute | solution.py:296
  145.0 8.1 %collective-permute-start.2 = (bf16[240,128]{1,0:T(8,128)(2,1)}, bf16[240,128]{1,0:T(8,128)(2,1)S(1)}, u32[]{:S(2)}, u32[]{:S(2)}) collective-permute-start(bf16[240,128]{1,0:T(8,128)(2,1)} %shard_map.146.refs_0_), channel_id=1, source_target_pairs={{0,7},{1,0},{2,1},{3,2},{4,3},{5,4},{6,5},{7,6},{8,15},{9,8},{10,9... | collective-permute-start | bytes 184328 | tf_op jit(solution)/shard_map/ppermute | solution.py:297
  151.0 26.2 %copy-start.9 = (f32[512]{0:T(512)S(1)}, f32[512]{0:T(512)}, u32[]{:S(2)}) copy-start(f32[512]{0:T(512)} %param.25) | copy-start | bytes 6148
  151.2 7.3 %collective-permute-start.1 = (bf16[240,128]{1,0:T(8,128)(2,1)S(1)}, bf16[240,128]{1,0:T(8,128)(2,1)S(1)}, u32[]{:S(2)}, u32[]{:S(2)}) collective-permute-start(bf16[240,128]{1,0:T(8,128)(2,1)S(1)} %collective-permute-done.refs_1_), channel_id=1, source_target_pairs={{0,1},{1,2},{2,3},{3,4},{4,5},{5,6},{6,7},{7,0},{8,9},{9,10},{10,1... | collective-permute-start | bytes 184328 | tf_op jit(solution)/shard_map/ppermute | solution.py:296
  153.1 6.1 %collective-permute-start.3 = (bf16[240,128]{1,0:T(8,128)(2,1)S(1)}, bf16[240,128]{1,0:T(8,128)(2,1)S(1)}, u32[]{:S(2)}, u32[]{:S(2)}) collective-permute-start(bf16[240,128]{1,0:T(8,128)(2,1)S(1)} %collective-permute-done.2.refs_5_), channel_id=1, source_target_pairs={{0,7},{1,0},{2,1},{3,2},{4,3},{5,4},{6,5},{7,6},{8,15},{9,8},{10,9... | collective-permute-start | bytes 184328 | tf_op jit(solution)/shard_map/ppermute | solution.py:297
  160.0 17.1 %all-to-all-start.4 = ((bf16[8,24,576]{2,1,0:T(8,128)(2,1)}), bf16[8,24,576]{2,1,0:T(8,128)(2,1)S(1)}, u32[]{:S(2)}, u32[]{:S(2)}) async-start(bf16[8,24,576]{2,1,0:T(8,128)(2,1)} %broadcast_in_dim.95), calls=%async_computation.6 | async-start | bytes 491520 | tf_op jit(solution)/shard_map/all_to_all | solution.py:31
  165.6 13.2 %collective-permute-start.4 = (bf16[240,128]{1,0:T(8,128)(2,1)S(1)}, bf16[240,128]{1,0:T(8,128)(2,1)S(1)}, u32[]{:S(2)}, u32[]{:S(2)}) collective-permute-start(bf16[240,128]{1,0:T(8,128)(2,1)S(1)} %collective-permute-done.1.refs_2_), channel_id=1, source_target_pairs={{0,1},{1,2},{2,3},{3,4},{4,5},{5,6},{6,7},{7,0},{8,9},{9,10},{10,1... | collective-permute-start | bytes 184328 | tf_op jit(solution)/shard_map/ppermute | solution.py:327
  168.9 9.8 %collective-permute-start.5 = (bf16[240,128]{1,0:T(8,128)(2,1)S(1)}, bf16[240,128]{1,0:T(8,128)(2,1)S(1)}, u32[]{:S(2)}, u32[]{:S(2)}) collective-permute-start(bf16[240,128]{1,0:T(8,128)(2,1)S(1)} %collective-permute-done.3.refs_6_), channel_id=1, source_target_pairs={{0,7},{1,0},{2,1},{3,2},{4,3},{5,4},{6,5},{7,6},{8,15},{9,8},{10,9... | collective-permute-start | bytes 184328 | tf_op jit(solution)/shard_map/ppermute | solution.py:329
  179.7 27.9 %all-to-all-start.5 = ((bf16[64,4,768]{2,1,0:T(4,128)(2,1)}), bf16[64,4,768]{2,1,0:T(4,128)(2,1)S(1)}, u32[]{:S(2)}, u32[]{:S(2)}) async-start(bf16[64,4,768]{2,1,0:T(4,128)(2,1)} %pad_maximum_fusion), calls=%async_computation.7 | async-start | bytes 786432 | tf_op jit(solution)/shard_map/all_to_all | solution.py:31
  193.2 15.5 %copy-start.1 = (bf16[240,128]{1,0:T(8,128)(2,1)S(1)}, bf16[240,128]{1,0:T(8,128)(2,1)}, u32[]{:S(2)}) copy-start(bf16[240,128]{1,0:T(8,128)(2,1)} %shard_map.146.refs_0_) | copy-start | bytes 184324
  193.7 15.0 %collective-permute-start.6 = (bf16[240,128]{1,0:T(8,128)(2,1)S(1)}, bf16[240,128]{1,0:T(8,128)(2,1)S(1)}, u32[]{:S(2)}, u32[]{:S(2)}) collective-permute-start(bf16[240,128]{1,0:T(8,128)(2,1)S(1)} %collective-permute-done.4.refs_3_), channel_id=1, source_target_pairs={{0,1},{1,2},{2,3},{3,4},{4,5},{5,6},{6,7},{7,0},{8,9},{9,10},{10,1... | collective-permute-start | bytes 184328 | tf_op jit(solution)/shard_map/ppermute | solution.py:327
Sparse Core Ops, SparseCore 0:
  34.8 42.4 all-gather.1
  82.6 41.8 reduce-scatter.4
  131.5 45.3 reduce-scatter.2

commit v3 on v2

--- a/solution.py
+++ b/solution.py
@@ -160,8 +160,11 @@
     ).astype(BF)
 
 
-def collect_kernel(x, out):
-    lines = x.shape[0]
+def collect_kernel(blocks, out, x, sem):
+    lines, lanes = x.shape
+    copy = pltpu.make_async_copy(blocks.at[:, pl.ds(blocks.shape[1] - lanes, lanes)], x, sem)
+    copy.start()
+    copy.wait()
     own = (
         lax.broadcasted_iota(jnp.int32, (ROWS, LANES), 1)
         == lax.broadcasted_iota(jnp.int32, (ROWS, LANES), 0) + (LAT - KVR)
@@ -281,14 +284,14 @@
         both, heads_axis * feats // 2, groups * CAP, w_gate, w_up, w_down, parts0
     )
 
-    pieces = both[:, heads_axis * feats // 2 :]
-    pieces, parts1 = together(pieces, parts1)
+    both, parts1 = together(both, parts1)
     pieces = pl.pallas_call(
         collect_kernel,
         out_shape=jax.ShapeDtypeStruct(((per + share) * rows, LANES), BF),
-        in_specs=[pl.BlockSpec(memory_space=pltpu.VMEM)],
+        in_specs=[pl.BlockSpec(memory_space=pltpu.HBM)],
         out_specs=pl.BlockSpec(memory_space=pltpu.VMEM),
-    )(pieces)
+        scratch_shapes=[pltpu.VMEM((groups * per, 2 * LANES), BF), pltpu.SemaphoreType.DMA],
+    )(both)
     right = [(i, (i + 1) % heads_axis) for i in range(heads_axis)]
     left = [(i, (i - 1) % heads_axis) for i in range(heads_axis)]
     ahead, behind = [pieces], [pieces]

time: 218 us -> 218 us (level)
  transfers between devices with their start and end apart: 15 -> 15, of which waited for: 8 -> 7; matrix products, arithmetic and copies ran while one was open for 7% -> 6% of each run, Pallas kernels for 8% -> 8%
where the time goes in v3:
time: 218 us; the launch traced here: 217 us
  waiting for transfers between devices  77.3 us (35%)
  starting transfers between devices  67.4 us (31%)
  blocking collectives  19.2 us (9%)
  Pallas kernels  18.4 us (8%)
  between operations  14.4 us (7%)
  local copies, waits for them, and re-layouts  10.3 us (5%)
  other arithmetic  7.24 us (3%)
  matrix products  3.14 us (1%)
    all_to_all x5, waiting for transfers between devices, exchange(): return lax.all_to_all(x, axis, split_axis=0, concat_axis=0, tiled=True)  65.5 us
    all_to_all x5, starting transfers between devices, exchange(): return lax.all_to_all(x, axis, split_axis=0, concat_axis=0, tiled=True)  45.7 us
    all_to_all x1, blocking collectives, exchange(): return lax.all_to_all(x, axis, split_axis=0, concat_axis=0, tiled=True)  19.2 us
    ppermute x3, starting transfers between devices, on_device(): behind.append(lax.ppermute(behind[-1], 'head', left))  12.5 us
    pallas_call x2, Pallas kernels, expert_part(): pl.pallas_call(kernel, out_shape=jax.ShapeDtypeStruct((count, feats), BF)...  11.8 us
    all_gather x1, waiting for transfers between devices, on_device(): lax.all_gather(arrived0.reshape(groups * CAP, feats), 'head', axis=1, til...  10.8 us
    ppermute x4, starting transfers between devices, on_device(): ahead.append(lax.ppermute(ahead[-1], 'head', right))  9.12 us
  transfers between devices with their start and end apart: 15, of which 7 were waited for; matrix products, arithmetic and copies ran while one was open for 6% of the time, Pallas kernels for 8%

profile of v3, /device:TPU:1, one launch (start us, length us, event | category | flops | bytes accessed | tf_op | source)
XLA Modules:
  0.0 217.4 jit_solution(6782974274321326470)
XLA Ops:
  7.2 0.8 slice_bitcast_fusion.3
  8.2 0.2 compare_reduce_fusion.1
  8.4 0.1 fusion.5
  8.5 1.0 convolution_convert_fusion
  9.5 0.8 reshape.976
  10.3 11.6 %all-to-all-start = ((bf16[64,4,512]{2,1,0:T(4,128)(2,1)}), bf16[64,4,512]{2,1,0:T(4,128)(2,1)S(1)}, u32[]{:S(2)}, u32[]{:S(2)}) async-start(bf16[64,4,512]{2,1,0:T(4,128)(2,1)} %reshape.976), calls=%async_computation | async-start | bytes 524288 | tf_op jit(solution)/shard_map/all_to_all | solution.py:31
  22.1 0.7 fusion.33
  22.8 0.7 fusion.34
  23.5 0.7 fusion.35
  24.3 0.7 fusion.36
  25.0 0.7 fusion.37
  25.8 8.2 %all-to-all-done = bf16[64,4,512]{2,1,0:T(4,128)(2,1)S(1)} async-done(((bf16[64,4,512]{2,1,0:T(4,128)(2,1)}), bf16[64,4,512]{2,1,0:T(4,128)(2,1)S(1)}, u32[]{:S(2)}, u32[]{:S(2)}) %all-to-all-start) | async-done | bytes 262176 | tf_op jit(solution)/shard_map/all_to_all | solution.py:31
  33.9 0.8 reshape.981
  35.1 0.1 copy.49
  35.3 0.1 copy.50
  35.5 0.1 broadcast_multiply_fusion
  35.7 0.1 fusion.23
  35.8 0.2 compare_reduce_fusion
  36.0 0.1 select_bitcast_fusion.1
  36.2 0.3 copy.48
  36.6 19.2 %all_to_all.30.tokens = bf16[8,24,512]{2,1,0:T(8,128)(2,1)S(1)} all-to-all(bf16[8,24,512]{2,1,0:T(8,128)(2,1)S(1)} %broadcast_in_dim.91), channel_id=1, replica_groups=mesh['expert'=64,'head'=8] {'head'}, dimensions={0} | all-to-all | bytes 393216 | tf_op jit(solution)/shard_map/all_to_all | solution.py:31
  55.8 2.7 %shard_map.143 = bf16[512,2304]{1,0:T(8,128)(2,1)} custom-call(bf16[2,512,24]{2,1,0:T(8,128)(2,1)S(1)} %stack.37.places, bf16[8,24,512]{2,1,0:T(8,128)(2,1)S(1)} %all_to_all.30.tokens, bf16[512,192]{1,0:T(8,128)(2,1)S(1)} %bitcast.62, bf16[192,256]{1,0:T(8,128)(2,1)S(1)} %bitcast.63), custom_call_target="tpu_custom_call" | custom-call | tf_op jit(solution)/shard_map/pallas_call | solution.py:270
  58.5 8.0 %all-to-all-start.2 = ((bf16[64,8,2304]{2,1,0:T(8,128)(2,1)}), bf16[64,8,2304]{2,1,0:T(8,128)(2,1)S(1)}, u32[]{:S(2)}, u32[]{:S(2)}) async-start(bf16[64,8,2304]{2,1,0:T(8,128)(2,1)} %bitcast.16), calls=%async_computation.2 | async-start | bytes 4718592 | tf_op jit(solution)/shard_map/all_to_all | solution.py:31
  66.6 10.8 %all-gather.2.cloned.1.call-done.refs_0_ = bf16[256,4096]{1,0:T(8,128)(2,1)} async-done(((bf16[256,512]{1,0:T(8,128)(2,1)}), bf16[256,4096]{1,0:T(8,128)(2,1)}) %all-gather.2.cloned.1.call-update) | async-done | bytes 2097168 | tf_op jit(solution)/shard_map/all_gather | solution.py:238
  77.3 5.1 %shard_map.144.refs_4_ = bf16[256,4096]{1,0:T(8,128)(2,1)} custom-call(bf16[256,4096]{1,0:T(8,128)(2,1)} %all-gather.2.cloned.1.call-done.refs_0_, bf16[1,4096,128]{2,1,0:T(8,128)(2,1)} %refs_1_.3, bf16[1,4096,128]{2,1,0:T(8,128)(2,1)} %refs_2_.3, bf16[1,128,4096]{2,1,0:T(8,128)(2,1)} %refs_3_.3), custom_call_target="tpu_custom_call" | custom-call | flops 805306368 | bytes 7340032 | tf_op jit(solution)/shard_map/pallas_call | solution.py:129
  82.5 40.6 %all-to-all-done.2 = bf16[64,8,2304]{2,1,0:T(8,128)(2,1)S(1)} async-done(((bf16[64,8,2304]{2,1,0:T(8,128)(2,1)}), bf16[64,8,2304]{2,1,0:T(8,128)(2,1)S(1)}, u32[]{:S(2)}, u32[]{:S(2)}) %all-to-all-start.2) | async-done | bytes 2359328 | tf_op jit(solution)/shard_map/all_to_all | solution.py:31
  123.2 1.4 copy-done.2
  124.6 6.7 %shard_map.145 = bf16[256,4096]{1,0:T(8,128)(2,1)} custom-call(bf16[512,2304]{1,0:T(8,128)(2,1)} %bitcast.64, bf16[1,4096,128]{2,1,0:T(8,128)(2,1)} %refs_1_.3, bf16[1,4096,128]{2,1,0:T(8,128)(2,1)} %refs_2_.3, bf16[1,128,4096]{2,1,0:T(8,128)(2,1)} %refs_3_.3, bf16[256,4096]{1,0:T(8,128)(2,1)} %shard_map.144.refs_4_), custom_call_target="tpu_custom_call" | custom-call | flops 805306368 | bytes 7340032 | tf_op jit(solution)/shard_map/pallas_call | solution.py:129
  131.3 0.7 copy-done.7
  132.2 1.7 reshape.983
  133.9 7.0 %all-to-all-start.3 = ((bf16[64,4,512]{2,1,0:T(4,128)(2,1)}), bf16[64,4,512]{2,1,0:T(4,128)(2,1)S(1)}, u32[]{:S(2)}, u32[]{:S(2)}) async-start(bf16[64,4,512]{2,1,0:T(4,128)(2,1)} %reshape.983), calls=%async_computation.5 | async-start | bytes 524288 | tf_op jit(solution)/shard_map/all_to_all | solution.py:31
  140.9 0.1 fusion.9
  141.0 2.2 shard_map.146.refs_0_
  143.2 1.9 collective-permute-start
  145.1 4.8 %collective-permute-start.2 = (bf16[240,128]{1,0:T(8,128)(2,1)}, bf16[240,128]{1,0:T(8,128)(2,1)S(1)}, u32[]{:S(2)}, u32[]{:S(2)}) collective-permute-start(bf16[240,128]{1,0:T(8,128)(2,1)} %shard_map.146.refs_0_), channel_id=1, source_target_pairs={{0,7},{1,0},{2,1},{3,2},{4,3},{5,4},{6,5},{7,6},{8,15},{9,8},{10,9... | collective-permute-start | bytes 184328 | tf_op jit(solution)/shard_map/ppermute | solution.py:300
  149.9 0.2 fusion.14
  150.1 0.2 broadcast_in_dim.84
  150.3 0.9 reshape.974
  151.2 0.2 collective-permute-done.refs_1_
  151.4 1.9 collective-permute-start.1
  153.3 4.6 %collective-permute-start.3 = (bf16[240,128]{1,0:T(8,128)(2,1)S(1)}, bf16[240,128]{1,0:T(8,128)(2,1)S(1)}, u32[]{:S(2)}, u32[]{:S(2)}) collective-permute-start(bf16[240,128]{1,0:T(8,128)(2,1)S(1)} %collective-permute-done.2.refs_5_), channel_id=1, source_target_pairs={{0,7},{1,0},{2,1},{3,2},{4,3},{5,4},{6,5},{7,6},{8,15},{9,8},{10,9... | collective-permute-start | bytes 184328 | tf_op jit(solution)/shard_map/ppermute | solution.py:300
  157.9 0.2 fusion.1
  158.2 0.3 convolution_convert_fusion.3
  158.5 0.7 collective-permute-done.3.refs_6_
  159.2 0.7 broadcast_in_dim.95
  159.9 5.1 %all-to-all-start.4 = ((bf16[8,24,576]{2,1,0:T(8,128)(2,1)}), bf16[8,24,576]{2,1,0:T(8,128)(2,1)S(1)}, u32[]{:S(2)}, u32[]{:S(2)}) async-start(bf16[8,24,576]{2,1,0:T(8,128)(2,1)} %broadcast_in_dim.95), calls=%async_computation.6 | async-start | bytes 491520 | tf_op jit(solution)/shard_map/all_to_all | solution.py:31
  165.1 0.4 fusion.78
  165.6 3.4 %collective-permute-start.4 = (bf16[240,128]{1,0:T(8,128)(2,1)S(1)}, bf16[240,128]{1,0:T(8,128)(2,1)S(1)}, u32[]{:S(2)}, u32[]{:S(2)}) collective-permute-start(bf16[240,128]{1,0:T(8,128)(2,1)S(1)} %collective-permute-done.1.refs_2_), channel_id=1, source_target_pairs={{0,1},{1,2},{2,3},{3,4},{4,5},{5,6},{6,7},{7,0},{8,9},{9,10},{10,1... | collective-permute-start | bytes 184328 | tf_op jit(solution)/shard_map/ppermute | solution.py:330
  168.9 3.1 %collective-permute-start.5 = (bf16[240,128]{1,0:T(8,128)(2,1)S(1)}, bf16[240,128]{1,0:T(8,128)(2,1)S(1)}, u32[]{:S(2)}, u32[]{:S(2)}) collective-permute-start(bf16[240,128]{1,0:T(8,128)(2,1)S(1)} %collective-permute-done.3.refs_6_), channel_id=1, source_target_pairs={{0,7},{1,0},{2,1},{3,2},{4,3},{5,4},{6,5},{7,6},{8,15},{9,8},{10,9... | collective-permute-start | bytes 184328 | tf_op jit(solution)/shard_map/ppermute | solution.py:332
  172.1 4.8 %all-to-all-done.4 = bf16[8,24,576]{2,1,0:T(8,128)(2,1)S(1)} async-done(((bf16[8,24,576]{2,1,0:T(8,128)(2,1)}), bf16[8,24,576]{2,1,0:T(8,128)(2,1)S(1)}, u32[]{:S(2)}, u32[]{:S(2)}) %all-to-all-start.4) | async-done | bytes 221216 | tf_op jit(solution)/shard_map/all_to_all | solution.py:31
  176.9 0.1 multiply_reduce_fusion
  177.1 0.3 convolution_convert_fusion.2
  177.5 1.0 reshape.982
  178.6 0.9 pad_maximum_fusion
  179.5 14.0 %all-to-all-start.5 = ((bf16[64,4,768]{2,1,0:T(4,128)(2,1)}), bf16[64,4,768]{2,1,0:T(4,128)(2,1)S(1)}, u32[]{:S(2)}, u32[]{:S(2)}) async-start(bf16[64,4,768]{2,1,0:T(4,128)(2,1)} %pad_maximum_fusion), calls=%async_computation.7 | async-start | bytes 786432 | tf_op jit(solution)/shard_map/all_to_all | solution.py:31
  193.5 0.2 fusion.12
  193.7 0.1 fusion.7
  193.8 0.3 convolution_convert_fusion.1.earlier
  194.2 1.9 collective-permute-start.6
  196.1 12.0 %all-to-all-done.5 = bf16[64,4,768]{2,1,0:T(4,128)(2,1)S(1)} async-done(((bf16[64,4,768]{2,1,0:T(4,128)(2,1)}), bf16[64,4,768]{2,1,0:T(4,128)(2,1)S(1)}, u32[]{:S(2)}, u32[]{:S(2)}) %all-to-all-start.5) | async-done | bytes 393248 | tf_op jit(solution)/shard_map/all_to_all | solution.py:31
  208.1 0.1 slice.74
  208.4 0.2 fusion.3
  208.6 0.6 pad_maximum_fusion.1
  209.2 1.7 shard_map.147
  (83 shorter events, 1.8 us)
Async XLA Ops:
  7.2 151.0 %copy-start = (bf16[512,576]{0,1:T(8,128)(2,1)S(1)}, bf16[512,576]{0,1:T(8,128)(2,1)}, u32[]{:S(2)}) copy-start(bf16[512,576]{0,1:T(8,128)(2,1)} %param.24) | copy-start | bytes 1769476
  7.2 27.6 %copy-start.6 = (s32[1,24]{1,0:T(1,128)S(1)}, s32[1,24]{1,0:T(1,128)}, u32[]{:S(2)}) copy-start(s32[1,24]{1,0:T(1,128)} %param.20) | copy-start | bytes 292
  7.2 28.0 %copy-start.10 = (s32[1,24]{1,0:T(1,128)S(1)}, s32[1,24]{1,0:T(1,128)}, u32[]{:S(2)}) copy-start(s32[1,24]{1,0:T(1,128)} %param.19) | copy-start | bytes 292
  7.2 28.0 %copy-start.8 = (s32[24]{0:T(128)S(1)}, s32[24]{0:T(128)}, u32[]{:S(2)}) copy-start(s32[24]{0:T(128)} %param.16) | copy-start | bytes 292
  7.2 28.2 %copy-start.3 = (bf16[24,16,576]{2,1,0:T(8,128)(2,1)S(1)}, bf16[24,16,576]{2,1,0:T(8,128)(2,1)}, u32[]{:S(2)}) copy-start(bf16[24,16,576]{2,1,0:T(8,128)(2,1)} %param.15) | copy-start | bytes 1327108
  9.5 27.0 %copy-start.5 = (bf16[2,24,512]{2,1,0:T(8,128)(2,1)S(1)}, bf16[2,24,512]{2,1,0:T(8,128)(2,1)}, u32[]{:S(2)}) copy-start(bf16[2,24,512]{2,1,0:T(8,128)(2,1)} %param.13) | copy-start | bytes 147460
  10.3 23.6 %all-to-all-start = ((bf16[64,4,512]{2,1,0:T(4,128)(2,1)}), bf16[64,4,512]{2,1,0:T(4,128)(2,1)S(1)}, u32[]{:S(2)}, u32[]{:S(2)}) async-start(bf16[64,4,512]{2,1,0:T(4,128)(2,1)} %reshape.976), calls=%async_computation | async-start | bytes 524288 | tf_op jit(solution)/shard_map/all_to_all | solution.py:31
  21.9 55.4 %all-gather.2.cloned.1.call-start = ((), (), s32[]{:S(2)}) async-start(), calls=%async_computation.8 | async-start | bytes 2359296 | tf_op jit(solution)/shard_map/all_gather | solution.py:238
  58.5 64.6 %all-to-all-start.2 = ((bf16[64,8,2304]{2,1,0:T(8,128)(2,1)}), bf16[64,8,2304]{2,1,0:T(8,128)(2,1)S(1)}, u32[]{:S(2)}, u32[]{:S(2)}) async-start(bf16[64,8,2304]{2,1,0:T(8,128)(2,1)} %bitcast.16), calls=%async_computation.2 | async-start | bytes 4718592 | tf_op jit(solution)/shard_map/all_to_all | solution.py:31
  66.5 65.7 %reduce-scatter.5.cloned.1.call-start = ((), (), s32[]{:S(2)}) async-start(), calls=%async_computation.10 | async-start | bytes 2359296 | tf_op jit(solution)/shard_map/reduce_scatter | solution.py:315
  82.5 95.1 %reduce-scatter.3.cloned.1.call-start = ((), (), s32[]{:S(2)}) async-start(), calls=%async_computation.9 | async-start | bytes 2359296 | tf_op jit(solution)/shard_map/reduce_scatter | solution.py:315
  123.2 1.4 copy-start.2
  131.3 0.7 copy-start.7
  131.3 9.7 %copy-start.4 = (bf16[2,24,8,576]{3,2,1,0:T(8,128)(2,1)S(1)}, bf16[2,24,8,576]{3,2,1,0:T(8,128)(2,1)}, u32[]{:S(2)}) copy-start(bf16[2,24,8,576]{3,2,1,0:T(8,128)(2,1)} %param.14) | copy-start | bytes 1327108
  133.9 24.0 %all-to-all-start.3 = ((bf16[64,4,512]{2,1,0:T(4,128)(2,1)}), bf16[64,4,512]{2,1,0:T(4,128)(2,1)S(1)}, u32[]{:S(2)}, u32[]{:S(2)}) async-start(bf16[64,4,512]{2,1,0:T(4,128)(2,1)} %reshape.983), calls=%async_computation.5 | async-start | bytes 524288 | tf_op jit(solution)/shard_map/all_to_all | solution.py:31
  143.2 8.2 %collective-permute-start = (bf16[240,128]{1,0:T(8,128)(2,1)}, bf16[240,128]{1,0:T(8,128)(2,1)S(1)}, u32[]{:S(2)}, u32[]{:S(2)}) collective-permute-start(bf16[240,128]{1,0:T(8,128)(2,1)} %shard_map.146.refs_0_), channel_id=1, source_target_pairs={{0,1},{1,2},{2,3},{3,4},{4,5},{5,6},{6,7},{7,0},{8,9},{9,10},{10,1... | collective-permute-start | bytes 184328 | tf_op jit(solution)/shard_map/ppermute | solution.py:299
  145.1 8.2 %collective-permute-start.2 = (bf16[240,128]{1,0:T(8,128)(2,1)}, bf16[240,128]{1,0:T(8,128)(2,1)S(1)}, u32[]{:S(2)}, u32[]{:S(2)}) collective-permute-start(bf16[240,128]{1,0:T(8,128)(2,1)} %shard_map.146.refs_0_), channel_id=1, source_target_pairs={{0,7},{1,0},{2,1},{3,2},{4,3},{5,4},{6,5},{7,6},{8,15},{9,8},{10,9... | collective-permute-start | bytes 184328 | tf_op jit(solution)/shard_map/ppermute | solution.py:300
  151.2 25.9 %copy-start.9 = (f32[512]{0:T(512)S(1)}, f32[512]{0:T(512)}, u32[]{:S(2)}) copy-start(f32[512]{0:T(512)} %param.25) | copy-start | bytes 6148
  151.4 7.1 %collective-permute-start.1 = (bf16[240,128]{1,0:T(8,128)(2,1)S(1)}, bf16[240,128]{1,0:T(8,128)(2,1)S(1)}, u32[]{:S(2)}, u32[]{:S(2)}) collective-permute-start(bf16[240,128]{1,0:T(8,128)(2,1)S(1)} %collective-permute-done.refs_1_), channel_id=1, source_target_pairs={{0,1},{1,2},{2,3},{3,4},{4,5},{5,6},{6,7},{7,0},{8,9},{9,10},{10,1... | collective-permute-start | bytes 184328 | tf_op jit(solution)/shard_map/ppermute | solution.py:299
  153.3 5.9 %collective-permute-start.3 = (bf16[240,128]{1,0:T(8,128)(2,1)S(1)}, bf16[240,128]{1,0:T(8,128)(2,1)S(1)}, u32[]{:S(2)}, u32[]{:S(2)}) collective-permute-start(bf16[240,128]{1,0:T(8,128)(2,1)S(1)} %collective-permute-done.2.refs_5_), channel_id=1, source_target_pairs={{0,7},{1,0},{2,1},{3,2},{4,3},{5,4},{6,5},{7,6},{8,15},{9,8},{10,9... | collective-permute-start | bytes 184328 | tf_op jit(solution)/shard_map/ppermute | solution.py:300
  159.9 16.9 %all-to-all-start.4 = ((bf16[8,24,576]{2,1,0:T(8,128)(2,1)}), bf16[8,24,576]{2,1,0:T(8,128)(2,1)S(1)}, u32[]{:S(2)}, u32[]{:S(2)}) async-start(bf16[8,24,576]{2,1,0:T(8,128)(2,1)} %broadcast_in_dim.95), calls=%async_computation.6 | async-start | bytes 491520 | tf_op jit(solution)/shard_map/all_to_all | solution.py:31
  165.6 13.0 %collective-permute-start.4 = (bf16[240,128]{1,0:T(8,128)(2,1)S(1)}, bf16[240,128]{1,0:T(8,128)(2,1)S(1)}, u32[]{:S(2)}, u32[]{:S(2)}) collective-permute-start(bf16[240,128]{1,0:T(8,128)(2,1)S(1)} %collective-permute-done.1.refs_2_), channel_id=1, source_target_pairs={{0,1},{1,2},{2,3},{3,4},{4,5},{5,6},{6,7},{7,0},{8,9},{9,10},{10,1... | collective-permute-start | bytes 184328 | tf_op jit(solution)/shard_map/ppermute | solution.py:330
  168.9 9.6 %collective-permute-start.5 = (bf16[240,128]{1,0:T(8,128)(2,1)S(1)}, bf16[240,128]{1,0:T(8,128)(2,1)S(1)}, u32[]{:S(2)}, u32[]{:S(2)}) collective-permute-start(bf16[240,128]{1,0:T(8,128)(2,1)S(1)} %collective-permute-done.3.refs_6_), channel_id=1, source_target_pairs={{0,7},{1,0},{2,1},{3,2},{4,3},{5,4},{6,5},{7,6},{8,15},{9,8},{10,9... | collective-permute-start | bytes 184328 | tf_op jit(solution)/shard_map/ppermute | solution.py:332
  179.5 28.6 %all-to-all-start.5 = ((bf16[64,4,768]{2,1,0:T(4,128)(2,1)}), bf16[64,4,768]{2,1,0:T(4,128)(2,1)S(1)}, u32[]{:S(2)}, u32[]{:S(2)}) async-start(bf16[64,4,768]{2,1,0:T(4,128)(2,1)} %pad_maximum_fusion), calls=%async_computation.7 | async-start | bytes 786432 | tf_op jit(solution)/shard_map/all_to_all | solution.py:31
  193.7 15.5 %copy-start.1 = (bf16[240,128]{1,0:T(8,128)(2,1)S(1)}, bf16[240,128]{1,0:T(8,128)(2,1)}, u32[]{:S(2)}) copy-start(bf16[240,128]{1,0:T(8,128)(2,1)} %shard_map.146.refs_0_) | copy-start | bytes 184324
  194.2 15.0 %collective-permute-start.6 = (bf16[240,128]{1,0:T(8,128)(2,1)S(1)}, bf16[240,128]{1,0:T(8,128)(2,1)S(1)}, u32[]{:S(2)}, u32[]{:S(2)}) collective-permute-start(bf16[240,128]{1,0:T(8,128)(2,1)S(1)} %collective-permute-done.4.refs_3_), channel_id=1, source_target_pairs={{0,1},{1,2},{2,3},{3,4},{4,5},{5,6},{6,7},{7,0},{8,9},{9,10},{10,1... | collective-permute-start | bytes 184328 | tf_op jit(solution)/shard_map/ppermute | solution.py:330
Sparse Core Ops, SparseCore 0:
  34.8 42.4 all-gather.1
  82.6 41.8 reduce-scatter.4
  131.4 45.1 reduce-scatter.2
